TPU v7x, 512 devices: a whole 4x4x16 slice. The times are simulated.
512 devices in a mesh: seq: 32 (over y_lo, z), mp: 16 (over x, y_hi, core).
Axes of the slice: x: 4, y: 4 (y_hi: 2, y_lo: 2; y = y_hi * 2 + y_lo), z: 16, core: 2. Of those that a mesh axis runs over, the one named last changes fastest.
Arguments:
- tokens: bfloat16 [8192, 2048], P('seq', 'mp'), may hold values from -6 to 6
- norm_gain: float32 [2048], replicated, may hold values from 0.1 to 1.9
- w_query: bfloat16 [2048, 2048], P('seq', 'mp'), may hold values from -0.75 to 0.75
- w_key: bfloat16 [2048, 2048], P('seq', 'mp'), may hold values from -0.75 to 0.75
- w_value: bfloat16 [2048, 2048], P('seq', 'mp'), may hold values from -0.125 to 0.125
- w_out: bfloat16 [2048, 2048], P('seq', 'mp'), may hold values from -0.125 to 0.125
- head_slope: float32 [16], replicated, may hold values from 0.01 to 0.5
- segment_ids: int32 [8192], P('seq'), may hold values from 0 to 31, never falling along the last dimension, each value on 1 to 1024 neighbouring positions
Outputs:
- mixed: bfloat16 [8192, 2048], P('seq', 'mp')
Inputs may be any that keep to these rules, and one draw needn't show every extreme that they name: `segment_ids`: homolog numbers never fall along the tokens; every number names 1 to 1024 consecutive tokens, and one names exactly 1024.
All inputs are finite; a program needn't handle non-finite values.
Results may differ from a plain program's by a relative error of at most 0.0055.
Values may be sent and summed in bfloat16 or wider, within the bound.
A program may use at most 64 MiB of HBM per device.

v0:
```python
import math

import jax
import jax.numpy as jnp
from jax import lax
from jax.sharding import PartitionSpec as P

D = 2048
HEADS = 16


EPSILON = 1e-05
MASKED_SCORE = -1e30


def make_carry(head_count, row_count, head_width):
    return (
        jnp.full((head_count, row_count), MASKED_SCORE, jnp.float32),
        jnp.zeros((head_count, row_count), jnp.float32),
        jnp.zeros((head_count, row_count, head_width), jnp.float32),
    )


def attend_block(
    running,
    query_rows,
    query_pos,
    query_seg,
    key_rows,
    value_rows,
    key_pos,
    key_seg,
    slopes,
    inv_scale,
):
    run_max, run_sum, run_acc = running
    scores = (
        jnp.einsum("qhd,khd->hqk", query_rows, key_rows, preferred_element_type=jnp.float32)
        * inv_scale
    )
    scores = scores - slopes[:, None, None] * (query_seg[:, None] - key_seg[None, :])[None]
    allowed = (key_pos[None, :] <= query_pos[:, None])[None]
    scores = jnp.where(allowed, scores, MASKED_SCORE)
    new_max = jnp.maximum(run_max, jnp.max(scores, axis=2))
    weights = jnp.where(allowed, jnp.exp(scores - new_max[:, :, None]), 0.0)
    factor = jnp.exp(run_max - new_max)
    new_sum = run_sum * factor + jnp.sum(weights, axis=2)
    weighted = jnp.einsum(
        "hqk,khd->hqd", weights.astype(jnp.bfloat16), value_rows, preferred_element_type=jnp.float32
    )
    return (new_max, new_sum, run_acc * factor[:, :, None] + weighted)


def fold_keys(carries, groups, key_rows, value_rows, key_seg, slopes, inv_scale):
    key_count = key_rows.shape[0]
    head_count = slopes.shape[0]
    block_rows = math.gcd(key_count, 512)
    key_blocks = key_rows.reshape(key_count // block_rows, block_rows, head_count, -1)
    value_blocks = value_rows.reshape(key_count // block_rows, block_rows, head_count, -1)
    seg_blocks = key_seg.astype(jnp.float32).reshape(key_count // block_rows, block_rows)

    def one_block(block_index, fold_state):
        key_pos = block_index * block_rows + lax.iota(jnp.int32, block_rows)
        key_part = key_blocks[block_index]
        value_part = value_blocks[block_index]
        seg_part = seg_blocks[block_index]
        updated = []
        for running, query_group in zip(fold_state, groups):
            query_rows, query_pos, query_seg = query_group

            def compute_part(current):
                return attend_block(
                    current,
                    query_rows,
                    query_pos,
                    query_seg,
                    key_part,
                    value_part,
                    key_pos,
                    seg_part,
                    slopes,
                    inv_scale,
                )

            def keep_part(current):
                return current

            updated.append(lax.cond(key_pos[0] <= query_pos[-1], compute_part, keep_part, running))
        return tuple(updated)

    return lax.fori_loop(0, key_count // block_rows, one_block, carries)


def finish(running):
    run_max, run_sum, run_acc = running
    result = run_acc / run_sum[:, :, None]
    head_count, row_count, head_width = result.shape
    return (
        jnp.transpose(result, (1, 0, 2))
        .reshape(row_count, head_count * head_width)
        .astype(jnp.bfloat16)
    )


def on_device(tokens, norm_gain, w_query, w_key, w_value, w_out, head_slope, segment_ids):
    row_count, local_width = tokens.shape
    seq_index = lax.axis_index("seq")
    mp_index = lax.axis_index("mp")
    head_width = D // HEADS
    local_heads = local_width // head_width
    inv_scale = 1.0 / math.sqrt(head_width)
    whole_rows = lax.all_gather(tokens, "mp", axis=1, tiled=True).astype(jnp.float32)
    mean_square = jnp.mean(whole_rows * whole_rows, axis=1, keepdims=True)
    normed = (whole_rows * lax.rsqrt(mean_square + EPSILON) * norm_gain).astype(jnp.bfloat16)
    pieces = (
        lax.all_gather(w_query, "seq", axis=0, tiled=True),
        lax.all_gather(w_key, "seq", axis=0, tiled=True),
        lax.all_gather(w_value, "seq", axis=0, tiled=True),
    )
    columns = normed
    query_sum, key_sum, value_sum = tuple(
        (
            jnp.dot(columns, weight_piece, preferred_element_type=jnp.float32)
            for weight_piece in pieces
        )
    )
    query_proj = query_sum.astype(jnp.bfloat16)
    key_proj = key_sum.astype(jnp.bfloat16)
    value_proj = value_sum.astype(jnp.bfloat16)
    slopes = lax.dynamic_slice_in_dim(head_slope, mp_index * local_heads, local_heads)
    own_pos = seq_index * row_count + lax.iota(jnp.int32, row_count)
    own_seg = segment_ids.astype(jnp.float32)
    key_seg = segment_ids.astype(jnp.bfloat16)
    query_rows = query_proj.reshape(row_count, local_heads, head_width)
    groups = ((query_rows, own_pos, own_seg),)
    pieces = (
        lax.all_gather(key_proj, "seq", axis=0, tiled=True),
        lax.all_gather(value_proj, "seq", axis=0, tiled=True),
        lax.all_gather(key_seg, "seq", axis=0, tiled=True),
    )
    fold_state = fold_keys(
        (make_carry(local_heads, row_count, head_width),),
        groups,
        pieces[0],
        pieces[1],
        pieces[2],
        slopes,
        inv_scale,
    )
    attended = finish(fold_state[0])
    gathered = lax.all_gather(attended, "mp", axis=1, tiled=True)
    columns = gathered
    projected = jnp.dot(
        columns,
        lax.all_gather(w_out, "seq", axis=0, tiled=True),
        preferred_element_type=jnp.float32,
    )
    return (tokens.astype(jnp.float32) + projected).astype(jnp.bfloat16)


def solution(mesh):
    return jax.shard_map(
        on_device,
        mesh=mesh,
        in_specs=(
            P("seq", "mp"),
            P(),
            P("seq", "mp"),
            P("seq", "mp"),
            P("seq", "mp"),
            P("seq", "mp"),
            P(),
            P("seq"),
        ),
        out_specs=P("seq", "mp"),
        check_vma=False,
    )
```

profile of v0, /device:TPU:2, one launch (start us, length us, event | category | flops | bytes accessed | tf_op | source)
XLA Modules:
  0.0 509.4 jit_solution(11352827320415788126)
XLA Ops:
  6.5 0.7 all-gather.7.cloned.1.call-update
  7.3 0.0 all-gather.9.cloned.1.call-start
  7.3 72.1 %all_gather.28 = bf16[2048,128]{1,0:T(8,128)(2,1)S(1)} all-gather(bf16[64,128]{1,0:T(8,128)(2,1)} %param.15), channel_id=1, replica_groups=mesh['seq'=32,'mp'=16] {'seq'}, dimensions={0}, use_global_device_ids=true | all-gather | bytes 540672 | tf_op jit(solution)/shard_map/all_gather | solution.py:117
  79.4 1.6 fusion.19
  81.0 2.4 convolution_convert_fusion.2
  83.4 0.0 all-gather.9.cloned.1.call-update
  83.4 0.0 all-gather.11.cloned.1.call-start
  83.5 61.9 %all_gather.32 = bf16[2048,128]{1,0:T(8,128)(2,1)S(1)} all-gather(bf16[64,128]{1,0:T(8,128)(2,1)S(1)} %copy-done.2), channel_id=1, replica_groups=mesh['seq'=32,'mp'=16] {'seq'}, dimensions={0}, use_global_device_ids=true | all-gather | bytes 540672 | tf_op jit(solution)/shard_map/all_gather | solution.py:118
  145.4 0.0 copy-done
  145.4 1.1 convolution_convert_fusion
  146.5 0.0 all-gather.11.cloned.1.call-update
  146.5 0.0 all-gather.13.cloned.1.call-start
  146.6 0.0 copy-done.5
  146.6 60.7 %all-gather.1 = bf16[32,1,256]{2,1,0:T(2,128)(2,1)S(1)} all-gather(bf16[1,1,256]{2,1,0:T(2,128)(2,1)S(1)} %reshape.115), channel_id=1, replica_groups=mesh['seq'=32,'mp'=16] {'seq'}, dimensions={0}, use_global_device_ids=true | all-gather | bytes 16896 | tf_op jit(solution)/shard_map/all_gather | solution.py:139
  207.3 0.1 convert_reduce_fusion
  207.4 0.0 copy-done.7
  207.4 0.6 dynamic_slice.45
  208.0 61.7 %all_gather.30 = bf16[2048,128]{1,0:T(8,128)(2,1)S(1)} all-gather(bf16[64,128]{1,0:T(8,128)(2,1)S(1)} %copy-done.3), channel_id=1, replica_groups=mesh['seq'=32,'mp'=16] {'seq'}, dimensions={0}, use_global_device_ids=true | all-gather | bytes 540672 | tf_op jit(solution)/shard_map/all_gather | solution.py:116
  269.8 0.5 fusion.23
  270.3 0.0 all-gather.9.cloned.1.call-done
  270.3 71.6 %all-gather.11.cloned.1.call-done = bf16[8192,128]{1,0:T(8,128)(2,1)} async-done(((bf16[256,128]{1,0:T(8,128)(2,1)}), bf16[8192,128]{1,0:T(8,128)(2,1)}) %all-gather.11.cloned.1.call-update) | async-done | bytes 2097168 | tf_op jit(solution)/shard_map/all_gather | solution.py:138
  341.9 0.0 copy-start.4
  341.9 0.0 copy-start.1
  341.9 43.2 %while.17 = (s32[]{:T(128)}, f32[1,256]{1,0:T(1,128)S(1)}, f32[1,256]{1,0:T(1,128)S(1)}, f32[1,256,128]{2,1,0:T(8,128)S(1)}, s32[256]{0:T(256)S(1)}, /*index=5*/...) while((s32[]{:T(128)}, f32[1,256]{1,0:T(1,128)S(1)}, ...), condition=%wide.region_6.7_spmd, body=%wide.region_1.6_spmd.sunk | while | flops 69141504 | bytes 2199375 | solution.py:91
  341.9 0.7 slice.17
  342.6 0.5 slice.16
  344.4 3.4 conditional.2
  344.4 1.8 fusion.28
  346.3 0.2 fusion.5
  346.4 1.3 fusion.3
  347.8 0.7 slice.17
  348.5 0.5 slice.16
  350.3 0.7 slice.17
  351.0 0.5 slice.16
  352.8 0.7 slice.17
  353.5 0.5 slice.16
  355.3 0.7 slice.17
  355.9 0.5 slice.16
  357.8 0.7 slice.17
  358.4 0.5 slice.16
  360.3 0.7 slice.17
  360.9 0.5 slice.16
  362.7 0.7 slice.17
  363.4 0.5 slice.16
  365.2 0.7 slice.17
  365.9 0.5 slice.16
  367.7 0.7 slice.17
  368.4 0.5 slice.16
  370.2 0.7 slice.17
  370.9 0.5 slice.16
  372.7 0.7 slice.17
  373.4 0.5 slice.16
  375.2 0.7 slice.17
  375.9 0.5 slice.16
  377.7 0.7 slice.17
  378.4 0.5 slice.16
  380.2 0.7 slice.17
  380.9 0.5 slice.16
  382.7 0.7 slice.17
  383.3 0.5 slice.16
  385.2 0.7 divide_convert_fusion
  385.9 0.0 all-gather.13.cloned.1.call-update
  385.9 114.7 %all_gather.35 = bf16[2048,128]{1,0:T(8,128)(2,1)S(1)} all-gather(bf16[64,128]{1,0:T(8,128)(2,1)S(1)} %copy-done.4), channel_id=1, replica_groups=mesh['seq'=32,'mp'=16] {'seq'}, dimensions={0}, use_global_device_ids=true | all-gather | bytes 540672 | tf_op jit(solution)/shard_map/all_gather | solution.py:155
  500.6 2.3 fusion.22
  (57 shorter events, 0.3 us)
Async XLA Ops:
  6.5 76.9 %copy-start.2 = (bf16[64,128]{1,0:T(8,128)(2,1)S(1)}, bf16[64,128]{1,0:T(8,128)(2,1)}, u32[]{:S(2)}) copy-start(bf16[64,128]{1,0:T(8,128)(2,1)} %param.16) | copy-start | bytes 49156
  6.5 72.9 %all-gather.7.cloned.1.call-start = ((), (), s32[]{:S(2)}) async-start(), calls=%async_computation | async-start | bytes 1114112 | tf_op jit(solution)/shard_map/all_gather | solution.py:112
  7.3 263.0 %all-gather.9.cloned.1.call-start = ((), (), s32[]{:S(2)}) async-start(), calls=%async_computation.1 | async-start | bytes 2162688 | tf_op jit(solution)/shard_map/all_gather | solution.py:137
  79.4 66.0 %copy-start.6 = (f32[2048]{0:T(1024)S(1)}, f32[2048]{0:T(1024)}, u32[]{:S(2)}) copy-start(f32[2048]{0:T(1024)} %param.13) | copy-start | bytes 24580
  79.4 66.0 %copy-start = (bf16[256,2048]{1,0:T(8,128)(2,1)S(1)}, bf16[256,2048]{1,0:T(8,128)(2,1)}, u32[]{:S(2)}) copy-start(bf16[256,2048]{1,0:T(8,128)(2,1)} %all-gather.7.cloned.1.call-done) | copy-start | bytes 3145732
  83.4 63.2 %copy-start.5 = (s32[256]{0:T(256)S(1)}, s32[256]{0:T(256)}, u32[]{:S(2)}) copy-start(s32[256]{0:T(256)} %param.19) | copy-start | bytes 3076
  83.4 124.0 %copy-start.7 = (f32[16]{0:T(128)S(1)}, f32[16]{0:T(128)}, u32[]{:S(2)}) copy-start(f32[16]{0:T(128)} %param.18) | copy-start | bytes 196
  83.4 124.7 %copy-start.3 = (bf16[64,128]{1,0:T(8,128)(2,1)S(1)}, bf16[64,128]{1,0:T(8,128)(2,1)}, u32[]{:S(2)}) copy-start(bf16[64,128]{1,0:T(8,128)(2,1)} %param.14) | copy-start | bytes 49156
  83.4 258.5 %all-gather.11.cloned.1.call-start = ((), (), s32[]{:S(2)}) async-start(), calls=%async_computation.2 | async-start | bytes 2162688 | tf_op jit(solution)/shard_map/all_gather | solution.py:138
  146.5 354.1 %all-gather.13.cloned.1.call-start = ((), (), s32[]{:S(2)}) async-start(), calls=%async_computation.3 | async-start | bytes 1114112 | tf_op jit(solution)/shard_map/all_gather | solution.py:151
  341.9 44.0 %copy-start.4 = (bf16[64,128]{1,0:T(8,128)(2,1)S(1)}, bf16[64,128]{1,0:T(8,128)(2,1)}, u32[]{:S(2)}) copy-start(bf16[64,128]{1,0:T(8,128)(2,1)} %param.17) | copy-start | bytes 49156
  341.9 158.7 %copy-start.1 = (bf16[256,128]{1,0:T(8,128)(2,1)S(1)}, bf16[256,128]{1,0:T(8,128)(2,1)}, u32[]{:S(2)}) copy-start(bf16[256,128]{1,0:T(8,128)(2,1)} %param.12) | copy-start | bytes 196612
Sparse Core Ops, SparseCore 0:
  10.5 65.0 all-gather.6
  83.5 129.4 all-gather.8
  215.1 126.7 all-gather.10
  386.0 103.0 all-gather.12
where the time goes:
time: 511 us; the launch traced here: 509 us
  blocking collectives  371 us (73%)
  waiting for transfers between devices  72.4 us (14%)
  loops' own time  20.9 us (4%)
  local copies, waits for them, and re-layouts  19.6 us (4%)
  between operations  13.2 us (3%)
  matrix products  9.41 us (2%)
    all_gather x1, blocking collectives, on_device(): lax.all_gather(w_out, 'seq', axis=0, tiled=True)  115 us
    all_gather x1, blocking collectives, on_device(): lax.all_gather(w_key, 'seq', axis=0, tiled=True)  72.1 us
    all_gather x1, waiting for transfers between devices, on_device(): lax.all_gather(value_proj, 'seq', axis=0, tiled=True)  71.6 us
    all_gather x1, blocking collectives, on_device(): lax.all_gather(w_value, 'seq', axis=0, tiled=True)  61.9 us
    all_gather x1, blocking collectives, on_device(): lax.all_gather(w_query, 'seq', axis=0, tiled=True)  61.7 us
    all_gather x1, blocking collectives, on_device(): lax.all_gather(key_seg, 'seq', axis=0, tiled=True)  60.7 us
    another operation x1, loops' own time, fold_keys(): return lax.fori_loop(0, key_count // block_rows, one_block, carries)  20.7 us
    slice x16, local copies, waits for them, and re-layouts, one_block(): query_pos[-1]  10.6 us
  transfers between devices with their start and end apart: 4, of which 1 were waited for; matrix products, arithmetic and copies ran while one was open for 0% of the time, Pallas kernels for 0%

commit v1 on v0

v1 whole, which is shorter than its diff:
```python
import functools
import math

import jax
import jax.numpy as jnp
from jax import lax
from jax.experimental import pallas as pl
from jax.experimental.pallas import tpu as pltpu
from jax.sharding import PartitionSpec as P

EPSILON = 1e-05
MASKED_SCORE = -1e30
MESH = pl.DeviceIdType.MESH


def remote(src, dst, send, recv, device):
    return pltpu.make_async_remote_copy(
        src_ref=src, dst_ref=dst, send_sem=send, recv_sem=recv, device_id=device, device_id_type=MESH
    )


def kernel(
    nz, nx, ny, tok, gain, wq, wk, wv, wo, slopes, seg, out,
    xg, nb, wg, kt, vb, qb, mb, lb, ab, ob, sb, att,
    tok_s, tok_r, w_s, w_r, wy_s, wy_r, k_s, k_r, v_s, v_r, x_s, x_r, a_s, a_r, f_s, f_r,
):
    rows, hw = tok.shape
    depth = wq.shape[0]
    nm = nx * ny * 2
    up_steps = nz // 2
    down_steps = nz - 1 - up_steps
    s = lax.axis_index("seq")
    m = lax.axis_index("mp")
    z = lax.rem(s, nz)
    yl = lax.div(s, nz)
    core = lax.rem(m, 2)
    yh = lax.rem(lax.div(m, 2), ny)
    x = lax.div(m, 2 * ny)

    def ring(place):
        return lax.rem(place + nz, nz)

    up = {"seq": yl * nz + ring(z + 1), "mp": m}
    down = {"seq": yl * nz + ring(z - 1), "mp": m}
    across = {"seq": (1 - yl) * nz + z, "mp": m}
    sibling = {"seq": s, "mp": m + 1 - 2 * core}

    def mp_at(index, sign, flip):
        a, b = index // ny, index % ny
        ox = lax.rem(x + (a if sign > 0 else nx - a), nx)
        oy = lax.rem(yh + (b if sign > 0 else ny - b), ny)
        oc = 1 - core if flip else core
        return (ox * ny + oy) * 2 + oc

    barrier = pltpu.get_barrier_semaphore()
    greeted = [up, down, across]
    for flip in (False, True):
        for index in range(nx * ny):
            if index or flip:
                greeted.append({"seq": s, "mp": mp_at(index, 1, flip)})
    for device in greeted:
        pl.semaphore_signal(barrier, inc=1, device_id=device, device_id_type=MESH)

    def shard(owner):
        return wg.at[pl.ds(pl.multiple_of(owner * depth, depth), depth), :]

    own_rows = pl.ds(pl.multiple_of(s * depth, depth), depth)
    for index, weight in enumerate((wq, wk, wv, wo)):
        wg[own_rows, index * hw:(index + 1) * hw] = weight[...]
    xg[m] = tok[...]
    pl.semaphore_wait(barrier, len(greeted))

    def w_up(step):
        ref = shard(yl * nz + ring(z - step + 1))
        return remote(ref, ref, w_s.at[0, step], w_r.at[0, step], up)

    def w_down(step):
        ref = shard(yl * nz + ring(z + step - 1))
        return remote(ref, ref, w_s.at[1, step], w_r.at[1, step], down)

    def w_across(way, step):
        ref = shard(yl * nz + ring(z - step if way == 0 else z + step))
        return remote(ref, ref, wy_s.at[way, step], wy_r.at[way, step], across)

    def w_across_in(way, step):
        ref = shard((1 - yl) * nz + ring(z - step if way == 0 else z + step))
        return remote(ref, ref, wy_s.at[way, step], wy_r.at[way, step], across)

    def w_up_in(step):
        ref = shard(yl * nz + ring(z - step))
        return remote(ref, ref, w_s.at[0, step], w_r.at[0, step], up)

    def w_down_in(step):
        ref = shard(yl * nz + ring(z + step))
        return remote(ref, ref, w_s.at[1, step], w_r.at[1, step], down)

    w_up(1).start()
    w_down(1).start()
    w_across(0, 0).start()

    partners = []
    for flip in (True, False):
        for index in range(nx * ny):
            if index or flip:
                partners.append((len(partners), index, flip))

    def tok_out(slot, index, flip):
        return remote(tok, xg.at[m], tok_s.at[slot], tok_r.at[slot], {"seq": s, "mp": mp_at(index, 1, flip)})

    def tok_in(slot, index, flip):
        ref = xg.at[mp_at(index, -1, flip)]
        return remote(ref, ref, tok_s.at[slot], tok_r.at[slot], sibling)

    for partner in partners:
        tok_out(*partner).start()

    def w_step(step, carry):
        w_up_in(step).wait_recv()

        @pl.when(step < up_steps)
        def _():
            w_up(step + 1).start()

        @pl.when(step <= down_steps)
        def _():
            w_down_in(step).wait_recv()

            @pl.when(step < down_steps)
            def _():
                w_down(step + 1).start()

        w_across(0, step).start()

        @pl.when(step <= down_steps)
        def _():
            w_across(1, step).start()

        return carry

    middle = up_steps // 2 + 1
    lax.fori_loop(1, middle + 1, w_step, 0)

    for partner in partners:
        tok_in(*partner).wait_recv()
    square = jnp.zeros((rows, hw), jnp.float32)
    for h in range(nm):
        part = xg[h].astype(jnp.float32)
        square = square + part * part
    mean = jnp.sum(square, axis=1, keepdims=True) * (1.0 / (nm * hw))
    scale = jnp.broadcast_to(lax.rsqrt(mean + EPSILON), (rows, hw))
    for h in range(nm):
        part = xg[h].astype(jnp.float32) * scale * gain[:, h * hw:(h + 1) * hw]
        nb[:, h * hw:(h + 1) * hw] = part.astype(jnp.bfloat16)

    lax.fori_loop(middle + 1, up_steps + 1, w_step, 0)

    def across_in(step, carry):
        w_across_in(0, step).wait_recv()

        @pl.when((step >= 1) & (step <= down_steps))
        def _():
            w_across_in(1, step).wait_recv()

        return carry

    lax.fori_loop(0, up_steps + 1, across_in, 0)

    proj = jnp.dot(nb[...], wg[:, :3 * hw], preferred_element_type=jnp.float32)
    qb[1] = proj[:, :hw].astype(jnp.bfloat16)
    kt[z, :hw, :] = jnp.transpose(proj[:, hw:2 * hw]).astype(jnp.bfloat16)
    kt[z, hw:hw + 16, :] = jnp.broadcast_to(seg[...].astype(jnp.float32), (16, rows)).astype(jnp.bfloat16)
    vb[z] = proj[:, 2 * hw:].astype(jnp.bfloat16)

    def kv_out(buf, ss, rs, way, step):
        ref = buf.at[ring(z - step + 1 if way == 0 else z + step - 1)]
        return remote(ref, ref, ss.at[way, step], rs.at[way, step], up if way == 0 else down)

    def kv_in(buf, ss, rs, way, step):
        ref = buf.at[ring(z - step if way == 0 else z + step)]
        return remote(ref, ref, ss.at[way, step], rs.at[way, step], up if way == 0 else down)

    key_side, value_side = (kt, k_s, k_r), (vb, v_s, v_r)
    for side in (key_side, value_side):
        kv_out(*side, 0, 1).start()
        kv_out(*side, 1, 1).start()

    query_copy = remote(qb.at[1], qb.at[0], x_s.at[0], x_r.at[0], across)

    @pl.when(yl == 1)
    def _():
        query_copy.start()

    slope = slopes[m]
    inv_scale = 1.0 / math.sqrt(hw)
    mb[...] = jnp.full(mb.shape, MASKED_SCORE, jnp.float32)
    lb[...] = jnp.zeros(lb.shape, jnp.float32)
    ab[...] = jnp.zeros(ab.shape, jnp.float32)

    def attend(group, block):
        bias = kt[block, hw:hw + 16, :].astype(jnp.float32)[:1, :] * slope
        scores = jnp.dot(qb[group], kt[block, :hw, :], preferred_element_type=jnp.float32)
        scores = scores * inv_scale + bias
        reach = jnp.where(group == 0, nz * rows, (z - block) * rows)
        row = lax.broadcasted_iota(jnp.int32, scores.shape, 0)
        col = lax.broadcasted_iota(jnp.int32, scores.shape, 1)
        scores = jnp.where(col - row <= reach, scores, MASKED_SCORE)
        old = mb[group]
        new = jnp.maximum(old, jnp.max(scores, axis=1, keepdims=True))
        weights = jnp.exp(scores - jnp.concatenate([new] * (rows // hw), axis=1))
        factor = jnp.exp(old - new)
        total = lb[group] * factor
        for part in range(rows // hw):
            total = total + weights[:, part * hw:(part + 1) * hw]
        mb[group] = new
        lb[group] = total
        ab[group] = ab[group] * factor + jnp.dot(
            weights.astype(jnp.bfloat16), vb[block], preferred_element_type=jnp.float32
        )

    def kv_step(step, carry):
        for side in (key_side, value_side):
            for way, last in ((0, up_steps), (1, down_steps)):
                @pl.when((step >= 1) & (step <= last))
                def _():
                    kv_in(*side, way, step).wait_recv()

                    @pl.when(step < last)
                    def _():
                        kv_out(*side, way, step + 1).start()

        def task(index, inner):
            way, group = lax.div(index, 2), 1 - lax.rem(index, 2)
            block = ring(jnp.where(way == 0, z - step, z + step))

            @pl.when((index == 1) & (step == 0) & (yl == 0))
            def _():
                query_copy.wait_recv()

            wanted = jnp.where(group == 0, yl == 0, block <= z)
            exists = (way == 0) | ((step >= 1) & (step <= down_steps))

            @pl.when(wanted & exists)
            def _():
                attend(group, block)

            return inner

        lax.fori_loop(0, 4, task, 0)

        w_across(0, step).wait_send()

        @pl.when(step >= 1)
        def _():
            w_up(step).wait_send()

        @pl.when((step >= 1) & (step <= down_steps))
        def _():
            w_down(step).wait_send()
            w_across(1, step).wait_send()

        return carry

    lax.fori_loop(0, up_steps + 1, kv_step, 0)

    out_copy = remote(ob.at[0], ob.at[1], x_s.at[1], x_r.at[1], across)
    stat_copy = remote(sb.at[0], sb.at[1], x_s.at[2], x_r.at[2], across)

    @pl.when(yl == 0)
    def _():
        total = jnp.sum(lb[0], axis=1, keepdims=True)
        ob[0] = (ab[0] / total).astype(jnp.bfloat16)
        level = jnp.broadcast_to(mb[0] + jnp.log(total), (rows, hw))
        sb[0] = jnp.transpose(level)[:8, :]
        out_copy.start()
        stat_copy.start()

    total = jnp.sum(lb[1], axis=1, keepdims=True)
    own = ab[1] / total

    @pl.when(yl == 0)
    def _():
        att[m] = own.astype(jnp.bfloat16)

    @pl.when(yl == 1)
    def _():
        out_copy.wait_recv()
        stat_copy.wait_recv()
        other_level = jnp.transpose(jnp.broadcast_to(sb[1][:1, :], (hw, rows)))
        own_level = jnp.broadcast_to(mb[1] + jnp.log(total), (rows, hw))
        share = 1.0 / (1.0 + jnp.exp(other_level - own_level))
        merged = own * share + ob[1].astype(jnp.float32) * (1.0 - share)
        att[m] = merged.astype(jnp.bfloat16)

    def att_out(index):
        ref = att.at[m]
        return remote(ref, ref, a_s.at[index], a_r.at[index], {"seq": s, "mp": mp_at(index, 1, False)})

    def att_in(index):
        ref = att.at[mp_at(index, -1, False)]
        return remote(ref, ref, a_s.at[index], a_r.at[index], sibling)

    def hand_out(index):
        ref = att.at[mp_at(index, -1, False)]
        return remote(ref, ref, f_s.at[index], f_r.at[index], sibling)

    def hand_in(index):
        ref = att.at[mp_at(index, -1, True)]
        return remote(ref, ref, f_s.at[index], f_r.at[index], sibling)

    chips = nx * ny
    for index in reversed(range(1, chips)):
        att_out(index).start()
    hand_out(0).start()

    def kv_sent(step, carry):
        for side in (key_side, value_side):
            kv_out(*side, 0, step).wait_send()

            @pl.when(step <= down_steps)
            def _():
                kv_out(*side, 1, step).wait_send()

        return carry

    lax.fori_loop(1, up_steps + 1, kv_sent, 0)
    for partner in partners:
        tok_out(*partner).wait_send()

    @pl.when(yl == 1)
    def _():
        query_copy.wait_send()

    @pl.when(yl == 0)
    def _():
        out_copy.wait_send()
        stat_copy.wait_send()

    for index in range(1, chips):
        att_in(index).wait_recv()
        hand_out(index).start()
    for index in range(chips):
        hand_in(index).wait_recv()

    mixed = tok[...].astype(jnp.float32)
    for pair in range(nm // 2):
        left = jnp.concatenate([att[2 * pair], att[2 * pair + 1]], axis=1)
        right = wg[2 * pair * hw:(2 * pair + 2) * hw, 3 * hw:]
        mixed = mixed + jnp.dot(left, right, preferred_element_type=jnp.float32)
    out[...] = mixed.astype(jnp.bfloat16)

    for index in range(1, chips):
        att_out(index).wait_send()
    for index in range(chips):
        hand_out(index).wait_send()


def on_device(nz, nx, ny, tokens, norm_gain, w_query, w_key, w_value, w_out, head_slope, segment_ids):
    rows, hw = tokens.shape
    depth = w_query.shape[0]
    nm = nx * ny * 2
    steps = nz // 2 + 1
    vmem = pl.BlockSpec(memory_space=pltpu.VMEM)
    dma = pltpu.SemaphoreType.DMA
    return pl.pallas_call(
        functools.partial(kernel, nz, nx, ny),
        out_shape=jax.ShapeDtypeStruct((rows, hw), jnp.bfloat16),
        in_specs=[vmem] * 6 + [pl.BlockSpec(memory_space=pltpu.SMEM), vmem],
        out_specs=vmem,
        scratch_shapes=[
            pltpu.VMEM((nm, rows, hw), jnp.bfloat16),
            pltpu.VMEM((rows, nm * hw), jnp.bfloat16),
            pltpu.VMEM((2 * nz * depth, 4 * hw), jnp.bfloat16),
            pltpu.VMEM((nz, hw + 16, rows), jnp.bfloat16),
            pltpu.VMEM((nz, rows, hw), jnp.bfloat16),
            pltpu.VMEM((2, rows, hw), jnp.bfloat16),
            pltpu.VMEM((2, rows, hw), jnp.float32),
            pltpu.VMEM((2, rows, hw), jnp.float32),
            pltpu.VMEM((2, rows, hw), jnp.float32),
            pltpu.VMEM((2, rows, hw), jnp.bfloat16),
            pltpu.VMEM((2, 8, rows), jnp.float32),
            pltpu.VMEM((nm, rows, hw), jnp.bfloat16),
            dma((nm - 1,)), dma((nm - 1,)),
            dma((2, steps)), dma((2, steps)),
            dma((2, steps)), dma((2, steps)),
            dma((2, steps)), dma((2, steps)),
            dma((2, steps)), dma((2, steps)),
            dma((3,)), dma((3,)),
            dma((nx * ny,)), dma((nx * ny,)),
            dma((nx * ny,)), dma((nx * ny,)),
        ],
        compiler_params=pltpu.CompilerParams(
            collective_id=0, has_side_effects=True, vmem_limit_bytes=40 << 20
        ),
        name="sublayer",
    )(
        tokens, norm_gain.reshape(1, -1), w_query, w_key, w_value, w_out, head_slope,
        segment_ids.reshape(1, -1),
    )


def solution(mesh):
    nz = mesh.shape["seq"] // 2
    ny = 2
    nx = mesh.shape["mp"] // (2 * ny)
    return jax.shard_map(
        functools.partial(on_device, nz, nx, ny),
        mesh=mesh,
        in_specs=(
            P("seq", "mp"), P(), P("seq", "mp"), P("seq", "mp"),
            P("seq", "mp"), P("seq", "mp"), P(), P("seq"),
        ),
        out_specs=P("seq", "mp"),
        check_vma=False,
    )
```

time: 511 us -> 104 us (0.20)
  the two profiles are of different devices: /device:TPU:2 before, /device:TPU:25 now
where the time goes in v1:
time: 104 us; the launch traced here: 103 us
  Pallas kernels  97.2 us (93%)
  local copies, waits for them, and re-layouts  5.72 us (6%)
    pallas_call x1, Pallas kernels, on_device(): pl.pallas_call(functools.partial(kernel, nz, nx, ny), out_shape=jax.Shape...  97.2 us
    unnamed x17, local copies, waits for them, and re-layouts  5.72 us

profile of v1, /device:TPU:25, one launch (start us, length us, event | category | flops | bytes accessed | tf_op | source)
XLA Modules:
  0.0 103.0 jit_solution(9478614373600824221)
XLA Ops:
  0.0 0.0 copy-start.6
  0.0 0.0 copy-start.7
  0.0 0.7 copy-done.6
  0.7 0.0 copy-done.7
  0.7 0.0 copy-start
  0.7 0.8 copy-done
  1.5 0.0 copy-start.1
  1.5 0.7 copy-done.1
  2.2 0.0 copy-start.2
  2.2 0.7 copy-done.2
  3.0 0.0 copy-start.3
  3.0 0.7 copy-done.3
  3.7 0.0 copy-start.4
  3.7 0.7 copy-done.4
  4.4 0.0 copy-start.5
  4.4 0.7 copy-done.5
  5.1 97.2 %sublayer.1 = bf16[256,128]{1,0:T(8,128)(2,1)S(1)} custom-call(bf16[256,128]{1,0:T(8,128)(2,1)S(1)} %copy-done, f32[1,2048]{1,0:T(1,128)S(1)} %bitcast.2, bf16[64,128]{1,0:T(8,128)(2,1)S(1)} %copy-done.1, bf16[64,128]{1,0:T(8,128)(2,1)S(1)} %copy-done.2, bf16[64,128]{1,0:T(8,128)(2,1)S(1)} %copy-done.3, bf16[64,128]{1,0:T(8,128)(2,1)S(1)} %copy-done.4, ...), custom_call_target="tpu_custom_call" | custom-call | tf_op jit(solution)/shard_map/sublayer/pallas_call | solution.py:364
  102.3 0.6 copy.10
Async XLA Ops:
  0.0 0.7 copy-start.6
  0.0 0.7 copy-start.7
  0.7 0.8 copy-start
  1.5 0.7 copy-start.1
  2.2 0.7 copy-start.2
  3.0 0.7 copy-start.3
  3.7 0.7 copy-start.4
  4.4 0.7 copy-start.5

commit v2 on v1

v2 whole, which is shorter than its diff:
```python
import functools
import math

import jax
import jax.numpy as jnp
from jax import lax
from jax.experimental import pallas as pl
from jax.experimental.pallas import tpu as pltpu
from jax.sharding import PartitionSpec as P

EPSILON = 1e-05
MASKED_SCORE = -1e30
MESH = pl.DeviceIdType.MESH


def remote(src, dst, send, recv, device):
    return pltpu.make_async_remote_copy(
        src_ref=src, dst_ref=dst, send_sem=send, recv_sem=recv, device_id=device, device_id_type=MESH
    )


def kernel(
    nz, nx, ny, tok, gain, wq, wk, wv, wo, slopes, seg, out,
    xg, nb, wg, gv, sv, kt, vb, qb, mb, lb, ab, ob, sb, att,
    l_s, o_s, o_r, tok_s, tok_r, w_s, w_r, wy_s, wy_r, kv_s, kv_r, x_s, x_r, a_s, a_r, f_s, f_r,
):
    rows, hw = tok.shape
    depth = wq.shape[0]
    nm = nx * ny * 2
    up_steps = nz // 2
    down_steps = nz - 1 - up_steps
    jump = 5
    s = lax.axis_index("seq")
    m = lax.axis_index("mp")
    z = lax.rem(s, nz)
    yl = lax.div(s, nz)
    core = lax.rem(m, 2)
    yh = lax.rem(lax.div(m, 2), ny)
    x = lax.div(m, 2 * ny)

    def ring(place):
        return lax.rem(place + nz, nz)

    def along(distance):
        return {"seq": yl * nz + ring(z + distance), "mp": m}

    up, down = along(1), along(-1)
    across = {"seq": (1 - yl) * nz + z, "mp": m}

    def tile(a, b, flip):
        return (lax.rem(x + a + nx, nx) * ny + lax.rem(yh + b, ny)) * 2 + (1 - core if flip else core)

    def row_device(a, b, flip):
        return {"seq": s, "mp": tile(a, b, flip)}

    sibling = row_device(0, 0, True)
    others = [(a, b) for a in range(nx) for b in range(ny) if a or b]

    barrier = pltpu.get_barrier_semaphore()
    greeted = [up, down, along(jump), along(-jump), across, sibling] + [row_device(a, b, False) for a, b in others]
    for device in greeted:
        pl.semaphore_signal(barrier, inc=1, device_id=device, device_id_type=MESH)

    def shard(row, owner):
        start = pl.multiple_of((row * nz + ring(owner)) * depth, depth)
        return wg.at[pl.ds(start, depth), :]

    own_rows = pl.ds(pl.multiple_of(s * depth, depth), depth)
    own_out = vb.at[z, pl.ds(pl.multiple_of(rows + yl * depth, depth), depth), :]
    loads = [
        pltpu.make_async_copy(wq, wg.at[own_rows, pl.ds(0, hw)], l_s.at[0]),
        pltpu.make_async_copy(wk, wg.at[own_rows, pl.ds(hw, hw)], l_s.at[1]),
        pltpu.make_async_copy(wv, wg.at[own_rows, pl.ds(2 * hw, hw)], l_s.at[2]),
        pltpu.make_async_copy(tok, xg.at[m], l_s.at[3]),
        pltpu.make_async_copy(wo, own_out, l_s.at[4]),
        pltpu.make_async_copy(gain, gv, l_s.at[5]),
        pltpu.make_async_copy(seg, sv, l_s.at[6]),
    ]
    for load in loads:
        load.start()
    mb[...] = jnp.full(mb.shape, MASKED_SCORE, jnp.float32)
    lb[...] = jnp.zeros(lb.shape, jnp.float32)
    ab[...] = jnp.zeros(ab.shape, jnp.float32)
    for load in loads:
        load.wait()
    pl.semaphore_wait(barrier, len(greeted))

    def w_send(way, offset):
        sign = 1 - 2 * way
        ref = shard(yl, z if offset in (1, jump) else z - sign * (offset - 1))
        device = along(sign * jump) if offset == jump else (up, down)[way]
        return remote(ref, ref, w_s.at[way, offset], w_r.at[way, offset], device)

    def w_arrival(way, offset):
        ref = shard(yl, z - (1 - 2 * way) * offset)
        return remote(ref, ref, w_s.at[way, offset], w_r.at[way, offset], up)

    def w_hand(way, offset):
        ref = shard(yl, z - (1 - 2 * way) * offset)
        return remote(ref, ref, wy_s.at[way, offset], wy_r.at[way, offset], across)

    def w_handed(way, offset):
        ref = shard(1 - yl, z - (1 - 2 * way) * offset)
        return remote(ref, ref, wy_s.at[way, offset], wy_r.at[way, offset], across)

    last_offset = (up_steps, down_steps)

    def w_event(offset):
        for way in (0, 1):
            if offset <= last_offset[way]:
                w_arrival(way, offset).wait_recv()
                if offset + 1 != jump and offset < last_offset[way]:
                    w_send(way, offset + 1).start()
                w_hand(way, offset).start()

    for way in (0, 1):
        w_send(way, 1).start()
    for way in (0, 1):
        w_send(way, jump).start()
    w_hand(0, 0).start()

    def tok_copy(slot, a, b, flip, device):
        index = (a * ny + b) * 2 + flip
        ref = xg.at[slot]
        return remote(ref, ref, tok_s.at[index], tok_r.at[index], device)

    def tok_arrival(a, b, flip):
        return tok_copy(tile(-a, b, flip), a, b, flip, sibling)

    tok_sends = [tok_copy(m, 0, 1, 0, row_device(0, 1, False))]
    tok_sends += [tok_copy(m, a, 0, 0, row_device(a, 0, False)) for a in range(1, nx)]
    tok_sends += [tok_copy(m, 0, 0, 1, sibling)]
    for copy in tok_sends:
        copy.start()
    out_weight = remote(own_out, own_out, o_s.at[0], o_r.at[0], across)
    out_weight.start()

    def tok_pass(a, b):
        tok_arrival(a, b, 0).wait_recv()
        later = []
        if (a, b) == (0, 1):
            later += [tok_copy(tile(0, 1, False), c, 1, 0, row_device(c, 0, False)) for c in range(1, nx)]
        later += [tok_copy(tile(-a, b, False), a, b, 1, sibling)]
        for copy in later:
            copy.start()
        tok_sends.extend(later)

    w_event(1)
    tok_pass(0, 1)
    w_event(2)
    for a in range(1, nx):
        tok_pass(a, 0)
    w_event(5)
    w_event(3)
    for a in range(1, nx):
        tok_pass(a, 1)
    w_event(6)
    w_event(4)
    w_event(7)

    for a, b in [(0, 0)] + others:
        tok_arrival(a, b, 1).wait_recv()
    square = jnp.zeros((rows, hw), jnp.float32)
    for h in range(nm):
        part = xg[h].astype(jnp.float32)
        square = square + part * part
    mean = jnp.sum(square, axis=1, keepdims=True) * (1.0 / (nm * hw))
    scale = jnp.broadcast_to(lax.rsqrt(mean + EPSILON), (rows, hw))
    for h in range(nm):
        part = xg[h].astype(jnp.float32) * scale * gv[:, h * hw:(h + 1) * hw]
        nb[:, h * hw:(h + 1) * hw] = part.astype(jnp.bfloat16)

    w_event(8)
    w_handed(0, 0).wait_recv()
    for offset in (1, 2, 5, 3, 6, 4, 7, 8):
        for way in (0, 1):
            if offset <= last_offset[way]:
                w_handed(way, offset).wait_recv()
    out_weight_in = vb.at[z, pl.ds(pl.multiple_of(rows + (1 - yl) * depth, depth), depth), :]
    remote(out_weight_in, out_weight_in, o_s.at[0], o_r.at[0], across).wait_recv()

    half = hw // 2
    middle = (rows + 2 * depth) // 2
    pieces = (
        (kt, 0, half), (kt, half, half + 16), (vb, 0, middle), (vb, middle, middle),
    )

    def kv_copy(piece, way, step, offset, device):
        buf, start, length = pieces[piece]
        ref = buf.at[ring(jnp.where(way == 0, z - offset, z + offset)), pl.ds(start, length), :]
        return remote(ref, ref, kv_s.at[piece, way], kv_r.at[piece, way, step], device)

    def kv_send(piece, way, step):
        return kv_copy(piece, way, step, step - 1, (up, down)[way])

    def kv_arrival(piece, way, step):
        return kv_copy(piece, way, step, step, (up, down)[way])

    proj = jnp.dot(nb[...], wg[:, hw:], preferred_element_type=jnp.float32)
    kt[z, :hw, :] = jnp.transpose(proj[:, :hw]).astype(jnp.bfloat16)
    kt[z, hw:hw + 16, :] = jnp.broadcast_to(sv[...].astype(jnp.float32), (16, rows)).astype(jnp.bfloat16)
    vb[z, :rows, :] = proj[:, hw:].astype(jnp.bfloat16)
    for piece in range(4):
        for way in (0, 1):
            kv_send(piece, way, 1).start()
    qb[1] = jnp.dot(nb[...], wg[:, :hw], preferred_element_type=jnp.float32).astype(jnp.bfloat16)
    query_copy = remote(qb.at[1], qb.at[0], x_s.at[0], x_r.at[0], across)

    @pl.when(yl == 1)
    def _():
        query_copy.start()

    slope = slopes[m]
    inv_scale = 1.0 / math.sqrt(hw)

    def attend(group, block):
        bias = kt[block, hw:hw + 16, :].astype(jnp.float32)[:1, :] * slope
        scores = jnp.dot(qb[group], kt[block, :hw, :], preferred_element_type=jnp.float32)
        scores = scores * inv_scale + bias
        reach = jnp.where(group == 0, nz * rows, (z - block) * rows)
        row = lax.broadcasted_iota(jnp.int32, scores.shape, 0)
        col = lax.broadcasted_iota(jnp.int32, scores.shape, 1)
        scores = jnp.where(col - row <= reach, scores, MASKED_SCORE)
        old = mb[group]
        new = jnp.maximum(old, jnp.max(scores, axis=1, keepdims=True))
        weights = jnp.exp(scores - jnp.concatenate([new] * (rows // hw), axis=1))
        factor = jnp.exp(old - new)
        total = lb[group] * factor
        for part in range(rows // hw):
            total = total + weights[:, part * hw:(part + 1) * hw]
        mb[group] = new
        lb[group] = total
        ab[group] = ab[group] * factor + jnp.dot(
            weights.astype(jnp.bfloat16), vb[block, :rows, :], preferred_element_type=jnp.float32
        )

    def kv_step(step, carry):
        def part(index, inner):
            for piece in range(4):
                for way in (0, 1):
                    @pl.when((index == piece) & (step <= last_offset[way]))
                    def _():
                        kv_arrival(piece, way, step).wait_recv()
                        kv_send(piece, way, step).wait_send()

                        @pl.when(step < last_offset[way])
                        def _():
                            kv_send(piece, way, step + 1).start()

            before = step - 1
            way, group = lax.div(index, 2), 1 - lax.rem(index, 2)
            block = ring(jnp.where(way == 0, z - before, z + before))

            @pl.when((index == 1) & (before == 0) & (yl == 0))
            def _():
                query_copy.wait_recv()

            wanted = jnp.where(group == 0, yl == 0, block <= z)
            exists = (way == 0) | ((before >= 1) & (before <= down_steps))

            @pl.when(wanted & exists)
            def _():
                attend(group, block)

            return inner

        return lax.fori_loop(0, 4, part, carry)

    lax.fori_loop(1, up_steps + 2, kv_step, 0)

    out_copy = remote(ob.at[0], ob.at[1], x_s.at[1], x_r.at[1], across)
    stat_copy = remote(sb.at[0], sb.at[1], x_s.at[2], x_r.at[2], across)

    @pl.when(yl == 0)
    def _():
        total = jnp.sum(lb[0], axis=1, keepdims=True)
        ob[0] = (ab[0] / total).astype(jnp.bfloat16)
        out_copy.start()
        level = jnp.broadcast_to(mb[0] + jnp.log(total), (rows, hw))
        sb[0] = jnp.transpose(level)[:8, :]
        stat_copy.start()

    total = jnp.sum(lb[1], axis=1, keepdims=True)
    own = ab[1] / total

    @pl.when(yl == 0)
    def _():
        att[m] = own.astype(jnp.bfloat16)

    @pl.when(yl == 1)
    def _():
        own_level = jnp.broadcast_to(mb[1] + jnp.log(total), (rows, hw))
        stat_copy.wait_recv()
        other_level = jnp.transpose(jnp.broadcast_to(sb[1][:1, :], (hw, rows)))
        share = 1.0 / (1.0 + jnp.exp(other_level - own_level))
        out_copy.wait_recv()
        merged = own * share + ob[1].astype(jnp.float32) * (1.0 - share)
        att[m] = merged.astype(jnp.bfloat16)

    def att_copy(slot, a, b, sems, device):
        ref = att.at[slot]
        return remote(ref, ref, sems[0].at[a * ny + b], sems[1].at[a * ny + b], device)

    direct, handed = (a_s, a_r), (f_s, f_r)
    att_sends = [att_copy(m, a, b, direct, row_device(a, b, False)) for a, b in reversed(others)]
    att_sends += [att_copy(m, 0, 0, handed, sibling)]
    for copy in att_sends:
        copy.start()

    for way in (0, 1):
        for offset in range(1, last_offset[way] + 1):
            w_send(way, offset).wait_send()
            w_hand(way, offset).wait_send()
    w_hand(0, 0).wait_send()
    out_weight.wait_send()
    for copy in tok_sends:
        copy.wait_send()

    @pl.when(yl == 1)
    def _():
        query_copy.wait_send()

    @pl.when(yl == 0)
    def _():
        out_copy.wait_send()
        stat_copy.wait_send()

    for a, b in others:
        att_copy(tile(-a, b, False), a, b, direct, sibling).wait_recv()
        copy = att_copy(tile(-a, b, False), a, b, handed, sibling)
        copy.start()
        att_sends.append(copy)
    for a, b in [(0, 0)] + others:
        att_copy(tile(-a, b, True), a, b, handed, sibling).wait_recv()

    mixed = xg[m].astype(jnp.float32)
    per_pair = 2 * hw // depth
    for pair in range(nm // 2):
        left = jnp.concatenate([att[2 * pair], att[2 * pair + 1]], axis=1)
        parts = []
        for owner in range(pair * per_pair, (pair + 1) * per_pair):
            start = rows + (owner // nz) * depth
            parts.append(vb[owner % nz, start:start + depth, :])
        mixed = mixed + jnp.dot(left, jnp.concatenate(parts, axis=0), preferred_element_type=jnp.float32)
    out[...] = mixed.astype(jnp.bfloat16)

    for copy in att_sends:
        copy.wait_send()


def on_device(nz, nx, ny, tokens, norm_gain, w_query, w_key, w_value, w_out, head_slope, segment_ids):
    rows, hw = tokens.shape
    depth = w_query.shape[0]
    nm = nx * ny * 2
    steps = nz // 2 + 1
    vmem = pl.BlockSpec(memory_space=pltpu.VMEM)
    hbm = pl.BlockSpec(memory_space=pltpu.HBM)
    dma = pltpu.SemaphoreType.DMA
    return pl.pallas_call(
        functools.partial(kernel, nz, nx, ny),
        out_shape=jax.ShapeDtypeStruct((rows, hw), jnp.bfloat16),
        in_specs=[hbm] * 6 + [pl.BlockSpec(memory_space=pltpu.SMEM), hbm],
        out_specs=vmem,
        scratch_shapes=[
            pltpu.VMEM((nm, rows, hw), jnp.bfloat16),
            pltpu.VMEM((rows, nm * hw), jnp.bfloat16),
            pltpu.VMEM((2 * nz * depth, 3 * hw), jnp.bfloat16),
            pltpu.VMEM((1, nm * hw), jnp.float32),
            pltpu.VMEM((1, rows), jnp.int32),
            pltpu.VMEM((nz, hw + 16, rows), jnp.bfloat16),
            pltpu.VMEM((nz, rows + 2 * depth, hw), jnp.bfloat16),
            pltpu.VMEM((2, rows, hw), jnp.bfloat16),
            pltpu.VMEM((2, rows, hw), jnp.float32),
            pltpu.VMEM((2, rows, hw), jnp.float32),
            pltpu.VMEM((2, rows, hw), jnp.float32),
            pltpu.VMEM((2, rows, hw), jnp.bfloat16),
            pltpu.VMEM((2, 8, rows), jnp.float32),
            pltpu.VMEM((nm, rows, hw), jnp.bfloat16),
            dma((7,)),
            dma((1,)), dma((1,)),
            dma((nm,)), dma((nm,)),
            dma((2, steps)), dma((2, steps)),
            dma((2, steps)), dma((2, steps)),
            dma((4, 2)), dma((4, 2, steps)),
            dma((3,)), dma((3,)),
            dma((nx * ny,)), dma((nx * ny,)),
            dma((nx * ny,)), dma((nx * ny,)),
        ],
        compiler_params=pltpu.CompilerParams(
            collective_id=0, has_side_effects=True, vmem_limit_bytes=60 << 20
        ),
        name="sublayer",
    )(
        tokens, norm_gain.reshape(1, -1), w_query, w_key, w_value, w_out, head_slope,
        segment_ids.reshape(1, -1),
    )


def solution(mesh):
    nz = mesh.shape["seq"] // 2
    ny = 2
    nx = mesh.shape["mp"] // (2 * ny)
    return jax.shard_map(
        functools.partial(on_device, nz, nx, ny),
        mesh=mesh,
        in_specs=(
            P("seq", "mp"), P(), P("seq", "mp"), P("seq", "mp"),
            P("seq", "mp"), P("seq", "mp"), P(), P("seq"),
        ),
        out_specs=P("seq", "mp"),
        check_vma=False,
    )
```

time: 104 us -> 91.3 us (0.88)
  Pallas kernels: 97.2 us -> 88.7 us
  local copies, waits for them, and re-layouts: 5.72 us -> 1.47 us
    pallas_call x1, Pallas kernels: 97.2 us -> 88.7 us  [on_device(): pl.pallas_call(functools.partial(kernel, nz, nx, ny), out_shape=jax.Shape...]
    unnamed x17 -> x1, local copies, waits for them, and re-layouts: 5.72 us -> 1.47 us
where the time goes in v2:
time: 91.3 us; the launch traced here: 90.2 us
  Pallas kernels  88.7 us (97%)
  local copies, waits for them, and re-layouts  1.47 us (2%)
    pallas_call x1, Pallas kernels, on_device(): pl.pallas_call(functools.partial(kernel, nz, nx, ny), out_shape=jax.Shape...  88.7 us

profile of v2, /device:TPU:25, one launch (start us, length us, event | category | flops | bytes accessed | tf_op | source)
XLA Modules:
  0.0 90.2 jit_solution(12235583617646979288)
XLA Ops:
  0.0 88.7 %sublayer.1 = bf16[256,128]{1,0:T(8,128)(2,1)} custom-call(bf16[256,128]{1,0:T(8,128)(2,1)} %tok.1, f32[1,2048]{1,0:T(1,128)} %bitcast.2, bf16[64,128]{1,0:T(8,128)(2,1)} %wq.1, bf16[64,128]{1,0:T(8,128)(2,1)} %wk.1, bf16[64,128]{1,0:T(8,128)(2,1)} %wv.1, bf16[64,128]{1,0:T(8,128)(2,1)} %wo.1, f32[16]{0:T(128)} %slopes.1, s32[1,256]{1,0:T(1,128)} %bitcast.3), custom_call_target="tpu_custom_call" | custom-call | tf_op jit(solution)/shard_map/sublayer/pallas_call | solution.py:359
  88.7 1.5 %copy.10 = bf16[256,128]{1,0:T(8,128)(2,1)} copy(bf16[256,128]{1,0:T(8,128)(2,1)} %sublayer.1) | data formatting | bytes 131072

commit v3 on v2

--- a/solution.py
+++ b/solution.py
@@ -21,8 +21,8 @@
 
 def kernel(
     nz, nx, ny, tok, gain, wq, wk, wv, wo, slopes, seg, out,
-    xg, nb, wg, gv, sv, kt, vb, qb, mb, lb, ab, ob, sb, att,
-    l_s, o_s, o_r, tok_s, tok_r, w_s, w_r, wy_s, wy_r, kv_s, kv_r, x_s, x_r, a_s, a_r, f_s, f_r,
+    xg, nb, wg, wog, gv, sv, kt, vb, qb, mb, lb, ab, ob, sb, att,
+    l_s, o_s, o_r, p_s, p_r, h_s, h_r, tok_s, tok_r, w_s, w_r, wy_r, kv_s, kv_r, x_s, x_r, a_s, a_r, f_s, f_r,
 ):
     rows, hw = tok.shape
     depth = wq.shape[0]
@@ -38,6 +38,9 @@
     yh = lax.rem(lax.div(m, 2), ny)
     x = lax.div(m, 2 * ny)
 
+    def arrived(ref, sem):
+        pltpu.make_async_copy(ref, ref, sem).wait()
+
     def ring(place):
         return lax.rem(place + nz, nz)
 
@@ -66,7 +69,7 @@
         return wg.at[pl.ds(start, depth), :]
 
     own_rows = pl.ds(pl.multiple_of(s * depth, depth), depth)
-    own_out = vb.at[z, pl.ds(pl.multiple_of(rows + yl * depth, depth), depth), :]
+    own_out = wog.at[z, yl]
     loads = [
         pltpu.make_async_copy(wq, wg.at[own_rows, pl.ds(0, hw)], l_s.at[0]),
         pltpu.make_async_copy(wk, wg.at[own_rows, pl.ds(hw, hw)], l_s.at[1]),
@@ -89,19 +92,15 @@
         sign = 1 - 2 * way
         ref = shard(yl, z if offset in (1, jump) else z - sign * (offset - 1))
         device = along(sign * jump) if offset == jump else (up, down)[way]
-        return remote(ref, ref, w_s.at[way, offset], w_r.at[way, offset], device)
+        return remote(ref, ref, w_s.at[0], w_r.at[way, offset], device)
 
     def w_arrival(way, offset):
         ref = shard(yl, z - (1 - 2 * way) * offset)
-        return remote(ref, ref, w_s.at[way, offset], w_r.at[way, offset], up)
+        return remote(ref, ref, w_s.at[0], w_r.at[way, offset], up)
 
     def w_hand(way, offset):
         ref = shard(yl, z - (1 - 2 * way) * offset)
-        return remote(ref, ref, wy_s.at[way, offset], wy_r.at[way, offset], across)
-
-    def w_handed(way, offset):
-        ref = shard(1 - yl, z - (1 - 2 * way) * offset)
-        return remote(ref, ref, wy_s.at[way, offset], wy_r.at[way, offset], across)
+        return remote(ref, ref, w_s.at[0], wy_r.at[0], across)
 
     last_offset = (up_steps, down_steps)
 
@@ -120,12 +119,9 @@
     w_hand(0, 0).start()
 
     def tok_copy(slot, a, b, flip, device):
-        index = (a * ny + b) * 2 + flip
         ref = xg.at[slot]
-        return remote(ref, ref, tok_s.at[index], tok_r.at[index], device)
-
-    def tok_arrival(a, b, flip):
-        return tok_copy(tile(-a, b, flip), a, b, flip, sibling)
+        kind = 3 if flip else 2 * b if a else 1
+        return remote(ref, ref, tok_s.at[0], tok_r.at[kind], device)
 
     tok_sends = [tok_copy(m, 0, 1, 0, row_device(0, 1, False))]
     tok_sends += [tok_copy(m, a, 0, 0, row_device(a, 0, False)) for a in range(1, nx)]
@@ -136,30 +132,30 @@
     out_weight.start()
 
     def tok_pass(a, b):
-        tok_arrival(a, b, 0).wait_recv()
         later = []
         if (a, b) == (0, 1):
             later += [tok_copy(tile(0, 1, False), c, 1, 0, row_device(c, 0, False)) for c in range(1, nx)]
         later += [tok_copy(tile(-a, b, False), a, b, 1, sibling)]
         for copy in later:
             copy.start()
-        tok_sends.extend(later)
 
     w_event(1)
+    arrived(xg.at[0], tok_r.at[1])
     tok_pass(0, 1)
     w_event(2)
+    arrived(xg.at[pl.ds(0, nx - 1)], tok_r.at[0])
     for a in range(1, nx):
         tok_pass(a, 0)
     w_event(5)
     w_event(3)
+    arrived(xg.at[pl.ds(0, nx - 1)], tok_r.at[2])
     for a in range(1, nx):
         tok_pass(a, 1)
     w_event(6)
     w_event(4)
     w_event(7)
 
-    for a, b in [(0, 0)] + others:
-        tok_arrival(a, b, 1).wait_recv()
+    arrived(xg.at[pl.ds(0, nx * ny)], tok_r.at[3])
     square = jnp.zeros((rows, hw), jnp.float32)
     for h in range(nm):
         part = xg[h].astype(jnp.float32)
@@ -171,24 +167,28 @@
         nb[:, h * hw:(h + 1) * hw] = part.astype(jnp.bfloat16)
 
     w_event(8)
-    w_handed(0, 0).wait_recv()
-    for offset in (1, 2, 5, 3, 6, 4, 7, 8):
-        for way in (0, 1):
-            if offset <= last_offset[way]:
-                w_handed(way, offset).wait_recv()
-    out_weight_in = vb.at[z, pl.ds(pl.multiple_of(rows + (1 - yl) * depth, depth), depth), :]
-    remote(out_weight_in, out_weight_in, o_s.at[0], o_r.at[0], across).wait_recv()
+    arrived(wg.at[pl.ds(0, nz * depth), :], wy_r.at[0])
+    other_out = wog.at[z, 1 - yl]
+    remote(other_out, other_out, o_s.at[0], o_r.at[0], across).wait_recv()
 
     half = hw // 2
-    middle = (rows + 2 * depth) // 2
+    middle = rows // 2
     pieces = (
         (kt, 0, half), (kt, half, half + 16), (vb, 0, middle), (vb, middle, middle),
     )
 
     def kv_copy(piece, way, step, offset, device):
         buf, start, length = pieces[piece]
-        ref = buf.at[ring(jnp.where(way == 0, z - offset, z + offset)), pl.ds(start, length), :]
-        return remote(ref, ref, kv_s.at[piece, way], kv_r.at[piece, way, step], device)
+        ref = buf.at[ring(z - (1 - 2 * way) * offset), pl.ds(start, length), :]
+        return remote(ref, ref, kv_s.at[piece, way], kv_r.at[piece, way, step - 1], device)
+
+    def kv_comes(way, step):
+        needed = z >= step if way == 0 else ring(z + step) < down_steps
+        return (step <= last_offset[way]) & ((yl == 0) | needed)
+
+    def kv_goes(way, step):
+        needed = (z >= step - 1) & (z < nz - 1) if way == 0 else ring(z + step - 1) < down_steps
+        return (step <= last_offset[way]) & ((yl == 0) | needed)
 
     def kv_send(piece, way, step):
         return kv_copy(piece, way, step, step - 1, (up, down)[way])
@@ -199,10 +199,13 @@
     proj = jnp.dot(nb[...], wg[:, hw:], preferred_element_type=jnp.float32)
     kt[z, :hw, :] = jnp.transpose(proj[:, :hw]).astype(jnp.bfloat16)
     kt[z, hw:hw + 16, :] = jnp.broadcast_to(sv[...].astype(jnp.float32), (16, rows)).astype(jnp.bfloat16)
-    vb[z, :rows, :] = proj[:, hw:].astype(jnp.bfloat16)
-    for piece in range(4):
-        for way in (0, 1):
-            kv_send(piece, way, 1).start()
+    vb[z] = proj[:, hw:].astype(jnp.bfloat16)
+    for way in (0, 1):
+        @pl.when(kv_goes(way, 1))
+        def _():
+            for piece in range(4):
+                kv_send(piece, way, 1).start()
+
     qb[1] = jnp.dot(nb[...], wg[:, :hw], preferred_element_type=jnp.float32).astype(jnp.bfloat16)
     query_copy = remote(qb.at[1], qb.at[0], x_s.at[0], x_r.at[0], across)
 
@@ -217,7 +220,7 @@
         bias = kt[block, hw:hw + 16, :].astype(jnp.float32)[:1, :] * slope
         scores = jnp.dot(qb[group], kt[block, :hw, :], preferred_element_type=jnp.float32)
         scores = scores * inv_scale + bias
-        reach = jnp.where(group == 0, nz * rows, (z - block) * rows)
+        reach = nz * rows if group == 0 else (z - block) * rows
         row = lax.broadcasted_iota(jnp.int32, scores.shape, 0)
         col = lax.broadcasted_iota(jnp.int32, scores.shape, 1)
         scores = jnp.where(col - row <= reach, scores, MASKED_SCORE)
@@ -231,40 +234,68 @@
         mb[group] = new
         lb[group] = total
         ab[group] = ab[group] * factor + jnp.dot(
-            weights.astype(jnp.bfloat16), vb[block, :rows, :], preferred_element_type=jnp.float32
+            weights.astype(jnp.bfloat16), vb[block], preferred_element_type=jnp.float32
         )
 
+    def wo_send(way, step):
+        ref = wog.at[ring(z - (1 - 2 * way) * (step - 1))]
+        return remote(ref, ref, p_s.at[way], p_r.at[way, step - 1], (up, down)[way])
+
+    def wo_step(way, step):
+        ref = wog.at[ring(z - (1 - 2 * way) * step)]
+        remote(ref, ref, p_s.at[way], p_r.at[way, step - 1], up).wait_recv()
+        remote(ref, ref, h_s.at[0], h_r.at[0], across).start()
+        wo_send(way, step).wait_send()
+
+        @pl.when(step < last_offset[way])
+        def _():
+            wo_send(way, step + 1).start()
+
+    @pl.when(yl == 1)
+    def _():
+        wo_send(0, 1).start()
+        wo_send(1, 1).start()
+
     def kv_step(step, carry):
-        def part(index, inner):
-            for piece in range(4):
-                for way in (0, 1):
-                    @pl.when((index == piece) & (step <= last_offset[way]))
-                    def _():
-                        kv_arrival(piece, way, step).wait_recv()
-                        kv_send(piece, way, step).wait_send()
-
-                        @pl.when(step < last_offset[way])
-                        def _():
-                            kv_send(piece, way, step + 1).start()
-
-            before = step - 1
-            way, group = lax.div(index, 2), 1 - lax.rem(index, 2)
-            block = ring(jnp.where(way == 0, z - before, z + before))
-
-            @pl.when((index == 1) & (before == 0) & (yl == 0))
-            def _():
-                query_copy.wait_recv()
-
-            wanted = jnp.where(group == 0, yl == 0, block <= z)
-            exists = (way == 0) | ((before >= 1) & (before <= down_steps))
-
-            @pl.when(wanted & exists)
+        before = step - 1
+        comes = [kv_comes(way, step) for way in (0, 1)]
+        went = [kv_goes(way, step) for way in (0, 1)]
+        goes = [kv_goes(way, step + 1) for way in (0, 1)]
+        for index in range(4):
+            for way in (0, 1):
+                @pl.when(comes[way])
+                def _():
+                    kv_arrival(index, way, step).wait_recv()
+
+                @pl.when(went[way])
+                def _():
+                    kv_send(index, way, step).wait_send()
+
+                @pl.when(goes[way])
+                def _():
+                    kv_send(index, way, step + 1).start()
+
+            way, group = index // 2, 1 - index % 2
+            block = ring(z - (1 - 2 * way) * before)
+            if index == 1:
+                @pl.when((before == 0) & (yl == 0))
+                def _():
+                    query_copy.wait_recv()
+
+            wanted = yl == 0 if group == 0 else block <= z
+            if way == 1:
+                wanted = wanted & (before >= 1) & (before <= down_steps)
+
+            @pl.when(wanted)
             def _():
                 attend(group, block)
 
-            return inner
-
-        return lax.fori_loop(0, 4, part, carry)
+        for way in (0, 1):
+            @pl.when((yl == 1) & (step <= last_offset[way]))
+            def _():
+                wo_step(way, step)
+
+        return carry
 
     lax.fori_loop(1, up_steps + 2, kv_step, 0)
 
@@ -299,7 +330,7 @@
 
     def att_copy(slot, a, b, sems, device):
         ref = att.at[slot]
-        return remote(ref, ref, sems[0].at[a * ny + b], sems[1].at[a * ny + b], device)
+        return remote(ref, ref, sems[0].at[0], sems[1].at[a * ny + b if sems is direct else 0], device)
 
     direct, handed = (a_s, a_r), (f_s, f_r)
     att_sends = [att_copy(m, a, b, direct, row_device(a, b, False)) for a, b in reversed(others)]
@@ -307,14 +338,17 @@
     for copy in att_sends:
         copy.start()
 
-    for way in (0, 1):
-        for offset in range(1, last_offset[way] + 1):
-            w_send(way, offset).wait_send()
-            w_hand(way, offset).wait_send()
-    w_hand(0, 0).wait_send()
+    arrived(wg.at[pl.ds(0, (2 * nz - 1) * depth), :], w_s.at[0])
+    arrived(xg.at[pl.ds(0, nm - 1)], tok_s.at[0])
     out_weight.wait_send()
-    for copy in tok_sends:
-        copy.wait_send()
+
+    @pl.when(yl == 1)
+    def _():
+        arrived(wog.at[pl.ds(0, nz - 1)], h_s.at[0])
+
+    @pl.when(yl == 0)
+    def _():
+        arrived(wog.at[pl.ds(0, nz - 1)], h_r.at[0])
 
     @pl.when(yl == 1)
     def _():
@@ -325,27 +359,26 @@
         out_copy.wait_send()
         stat_copy.wait_send()
 
+    per_head = hw // depth
+
+    def project(head):
+        first = head * per_head
+        weight = wog[pl.ds(lax.rem(first, nz), per_head), lax.div(first, nz)].reshape(hw, hw)
+        return jnp.dot(att[head], weight, preferred_element_type=jnp.float32)
+
+    mixed = xg[m].astype(jnp.float32) + project(m)
     for a, b in others:
-        att_copy(tile(-a, b, False), a, b, direct, sibling).wait_recv()
-        copy = att_copy(tile(-a, b, False), a, b, handed, sibling)
-        copy.start()
-        att_sends.append(copy)
+        head = tile(-a, b, False)
+        att_copy(head, a, b, direct, sibling).wait_recv()
+        att_copy(head, a, b, handed, sibling).start()
+        mixed = mixed + project(head)
+    arrived(att.at[pl.ds(0, nx * ny)], f_r.at[0])
     for a, b in [(0, 0)] + others:
-        att_copy(tile(-a, b, True), a, b, handed, sibling).wait_recv()
-
-    mixed = xg[m].astype(jnp.float32)
-    per_pair = 2 * hw // depth
-    for pair in range(nm // 2):
-        left = jnp.concatenate([att[2 * pair], att[2 * pair + 1]], axis=1)
-        parts = []
-        for owner in range(pair * per_pair, (pair + 1) * per_pair):
-            start = rows + (owner // nz) * depth
-            parts.append(vb[owner % nz, start:start + depth, :])
-        mixed = mixed + jnp.dot(left, jnp.concatenate(parts, axis=0), preferred_element_type=jnp.float32)
+        mixed = mixed + project(tile(-a, b, True))
     out[...] = mixed.astype(jnp.bfloat16)
 
-    for copy in att_sends:
-        copy.wait_send()
+    arrived(att.at[pl.ds(0, nx * ny - 1)], a_s.at[0])
+    arrived(att.at[pl.ds(0, nx * ny)], f_s.at[0])
 
 
 def on_device(nz, nx, ny, tokens, norm_gain, w_query, w_key, w_value, w_out, head_slope, segment_ids):
@@ -365,10 +398,11 @@
             pltpu.VMEM((nm, rows, hw), jnp.bfloat16),
             pltpu.VMEM((rows, nm * hw), jnp.bfloat16),
             pltpu.VMEM((2 * nz * depth, 3 * hw), jnp.bfloat16),
+            pltpu.VMEM((nz, 2, depth, hw), jnp.bfloat16),
             pltpu.VMEM((1, nm * hw), jnp.float32),
             pltpu.VMEM((1, rows), jnp.int32),
             pltpu.VMEM((nz, hw + 16, rows), jnp.bfloat16),
-            pltpu.VMEM((nz, rows + 2 * depth, hw), jnp.bfloat16),
+            pltpu.VMEM((nz, rows, hw), jnp.bfloat16),
             pltpu.VMEM((2, rows, hw), jnp.bfloat16),
             pltpu.VMEM((2, rows, hw), jnp.float32),
             pltpu.VMEM((2, rows, hw), jnp.float32),
@@ -378,13 +412,15 @@
             pltpu.VMEM((nm, rows, hw), jnp.bfloat16),
             dma((7,)),
             dma((1,)), dma((1,)),
-            dma((nm,)), dma((nm,)),
-            dma((2, steps)), dma((2, steps)),
-            dma((2, steps)), dma((2, steps)),
-            dma((4, 2)), dma((4, 2, steps)),
+            dma((2,)), dma((2, steps - 1)),
+            dma((1,)), dma((1,)),
+            dma((1,)), dma((4,)),
+            dma((1,)), dma((2, steps)),
+            dma((1,)),
+            dma((4, 2)), dma((4, 2, steps - 1)),
             dma((3,)), dma((3,)),
-            dma((nx * ny,)), dma((nx * ny,)),
-            dma((nx * ny,)), dma((nx * ny,)),
+            dma((1,)), dma((nx * ny,)),
+            dma((1,)), dma((1,)),
         ],
         compiler_params=pltpu.CompilerParams(
             collective_id=0, has_side_effects=True, vmem_limit_bytes=60 << 20

time: 91.3 us -> 87.2 us (0.955)
  Pallas kernels: 88.7 us -> 85.2 us
    pallas_call x1, Pallas kernels: 88.7 us -> 85.2 us  [on_device(): pl.pallas_call(functools.partial(kernel, nz, nx, ny), out_shape=jax.Shape...]
where the time goes in v3:
time: 87.2 us; the launch traced here: 86.6 us
  Pallas kernels  85.2 us (98%)
  local copies, waits for them, and re-layouts  1.47 us (2%)
    pallas_call x1, Pallas kernels, on_device(): pl.pallas_call(functools.partial(kernel, nz, nx, ny), out_shape=jax.Shape...  85.2 us

profile of v3, /device:TPU:25, one launch (start us, length us, event | category | flops | bytes accessed | tf_op | source)
XLA Modules:
  0.0 86.6 jit_solution(14557934851864337464)
XLA Ops:
  0.0 85.2 %sublayer.1 = bf16[256,128]{1,0:T(8,128)(2,1)} custom-call(bf16[256,128]{1,0:T(8,128)(2,1)} %tok.1, f32[1,2048]{1,0:T(1,128)} %bitcast.2, bf16[64,128]{1,0:T(8,128)(2,1)} %wq.1, bf16[64,128]{1,0:T(8,128)(2,1)} %wk.1, bf16[64,128]{1,0:T(8,128)(2,1)} %wv.1, bf16[64,128]{1,0:T(8,128)(2,1)} %wo.1, f32[16]{0:T(128)} %slopes.1, s32[1,256]{1,0:T(1,128)} %bitcast.3), custom_call_target="tpu_custom_call" | custom-call | tf_op jit(solution)/shard_map/sublayer/pallas_call | solution.py:392
  85.2 1.5 %copy.10 = bf16[256,128]{1,0:T(8,128)(2,1)} copy(bf16[256,128]{1,0:T(8,128)(2,1)} %sublayer.1) | data formatting | bytes 131072

commit v4 on v3

--- a/solution.py
+++ b/solution.py
@@ -21,15 +21,15 @@
 
 def kernel(
     nz, nx, ny, tok, gain, wq, wk, wv, wo, slopes, seg, out,
-    xg, nb, wg, wog, gv, sv, kt, vb, qb, mb, lb, ab, ob, sb, att,
-    l_s, o_s, o_r, p_s, p_r, h_s, h_r, tok_s, tok_r, w_s, w_r, wy_r, kv_s, kv_r, x_s, x_r, a_s, a_r, f_s, f_r,
+    xg, nb, wg, wgq, wog, gv, sv, kt, vb, qb, mb, lb, ab, ob, sb, att,
+    l_s, o_s, o_r, p_s, p_r, h_s, h_r, tok_s, tok_r, w_s, w_r, wy_r, q_s, q_r, qy_r, kv_s, kv_r, x_s, x_r, a_s, a_r, f_s, f_r,
 ):
     rows, hw = tok.shape
     depth = wq.shape[0]
     nm = nx * ny * 2
     up_steps = nz // 2
     down_steps = nz - 1 - up_steps
-    jump = 5
+    stride = 2
     s = lax.axis_index("seq")
     m = lax.axis_index("mp")
     z = lax.rem(s, nz)
@@ -60,20 +60,20 @@
     others = [(a, b) for a in range(nx) for b in range(ny) if a or b]
 
     barrier = pltpu.get_barrier_semaphore()
-    greeted = [up, down, along(jump), along(-jump), across, sibling] + [row_device(a, b, False) for a, b in others]
+    greeted = [along(way * far) for far in range(1, stride + 1) for way in (1, -1)] + [across, sibling] + [row_device(a, b, False) for a, b in others]
     for device in greeted:
         pl.semaphore_signal(barrier, inc=1, device_id=device, device_id_type=MESH)
 
-    def shard(row, owner):
+    def shard(buf, row, owner):
         start = pl.multiple_of((row * nz + ring(owner)) * depth, depth)
-        return wg.at[pl.ds(start, depth), :]
+        return buf.at[pl.ds(start, depth), :]
 
     own_rows = pl.ds(pl.multiple_of(s * depth, depth), depth)
     own_out = wog.at[z, yl]
     loads = [
-        pltpu.make_async_copy(wq, wg.at[own_rows, pl.ds(0, hw)], l_s.at[0]),
-        pltpu.make_async_copy(wk, wg.at[own_rows, pl.ds(hw, hw)], l_s.at[1]),
-        pltpu.make_async_copy(wv, wg.at[own_rows, pl.ds(2 * hw, hw)], l_s.at[2]),
+        pltpu.make_async_copy(wq, wgq.at[own_rows, :], l_s.at[0]),
+        pltpu.make_async_copy(wk, wg.at[own_rows, pl.ds(0, hw)], l_s.at[1]),
+        pltpu.make_async_copy(wv, wg.at[own_rows, pl.ds(hw, hw)], l_s.at[2]),
         pltpu.make_async_copy(tok, xg.at[m], l_s.at[3]),
         pltpu.make_async_copy(wo, own_out, l_s.at[4]),
         pltpu.make_async_copy(gain, gv, l_s.at[5]),
@@ -88,35 +88,36 @@
         load.wait()
     pl.semaphore_wait(barrier, len(greeted))
 
-    def w_send(way, offset):
+    key_value, queries = (wg, w_s, w_r, wy_r), (wgq, q_s, q_r, qy_r)
+
+    def w_send(side, way, offset):
+        buf, sent, came, _ = side
         sign = 1 - 2 * way
-        ref = shard(yl, z if offset in (1, jump) else z - sign * (offset - 1))
-        device = along(sign * jump) if offset == jump else (up, down)[way]
-        return remote(ref, ref, w_s.at[0], w_r.at[way, offset], device)
-
-    def w_arrival(way, offset):
-        ref = shard(yl, z - (1 - 2 * way) * offset)
-        return remote(ref, ref, w_s.at[0], w_r.at[way, offset], up)
-
-    def w_hand(way, offset):
-        ref = shard(yl, z - (1 - 2 * way) * offset)
-        return remote(ref, ref, w_s.at[0], wy_r.at[0], across)
+        hops = min(offset, stride)
+        ref = shard(buf, yl, z - sign * (offset - hops))
+        return remote(ref, ref, sent.at[0], came.at[way, offset], along(sign * hops))
+
+    def w_hand(side, way, offset):
+        buf, sent, _, handed = side
+        ref = shard(buf, yl, z - (1 - 2 * way) * offset)
+        return remote(ref, ref, sent.at[0], handed.at[0], across)
+
+    def w_event(offset, sides=None):
+        for side in sides or (key_value, queries):
+            for way in (0, 1):
+                if offset <= last_offset[way]:
+                    arrived(shard(side[0], yl, z - (1 - 2 * way) * offset), side[2].at[way, offset])
+                    if offset + stride <= last_offset[way]:
+                        w_send(side, way, offset + stride).start()
+                    w_hand(side, way, offset).start()
 
     last_offset = (up_steps, down_steps)
-
-    def w_event(offset):
-        for way in (0, 1):
-            if offset <= last_offset[way]:
-                w_arrival(way, offset).wait_recv()
-                if offset + 1 != jump and offset < last_offset[way]:
-                    w_send(way, offset + 1).start()
-                w_hand(way, offset).start()
-
-    for way in (0, 1):
-        w_send(way, 1).start()
-    for way in (0, 1):
-        w_send(way, jump).start()
-    w_hand(0, 0).start()
+    for first in range(1, stride + 1):
+        for side in (key_value, queries):
+            for way in (0, 1):
+                w_send(side, way, first).start()
+    for side in (key_value, queries):
+        w_hand(side, 0, 0).start()
 
     def tok_copy(slot, a, b, flip, device):
         ref = xg.at[slot]
@@ -139,22 +140,24 @@
         for copy in later:
             copy.start()
 
-    w_event(1)
+    w_event(1, (key_value,))
+    w_event(2, (key_value,))
     arrived(xg.at[0], tok_r.at[1])
     tok_pass(0, 1)
-    w_event(2)
     arrived(xg.at[pl.ds(0, nx - 1)], tok_r.at[0])
     for a in range(1, nx):
         tok_pass(a, 0)
-    w_event(5)
-    w_event(3)
+    w_event(1, (queries,))
+    w_event(2, (queries,))
+    w_event(3, (key_value,))
+    w_event(4, (key_value,))
     arrived(xg.at[pl.ds(0, nx - 1)], tok_r.at[2])
     for a in range(1, nx):
         tok_pass(a, 1)
-    w_event(6)
-    w_event(4)
-    w_event(7)
-
+    w_event(3, (queries,))
+    w_event(4, (queries,))
+    w_event(5, (key_value,))
+    w_event(6, (key_value,))
     arrived(xg.at[pl.ds(0, nx * ny)], tok_r.at[3])
     square = jnp.zeros((rows, hw), jnp.float32)
     for h in range(nm):
@@ -166,10 +169,13 @@
         part = xg[h].astype(jnp.float32) * scale * gv[:, h * hw:(h + 1) * hw]
         nb[:, h * hw:(h + 1) * hw] = part.astype(jnp.bfloat16)
 
-    w_event(8)
+    w_event(5, (queries,))
+    w_event(6, (queries,))
+    w_event(7, (key_value,))
+    w_event(8, (key_value,))
+    w_event(7, (queries,))
+    w_event(8, (queries,))
     arrived(wg.at[pl.ds(0, nz * depth), :], wy_r.at[0])
-    other_out = wog.at[z, 1 - yl]
-    remote(other_out, other_out, o_s.at[0], o_r.at[0], across).wait_recv()
 
     half = hw // 2
     middle = rows // 2
@@ -196,7 +202,7 @@
     def kv_arrival(piece, way, step):
         return kv_copy(piece, way, step, step, (up, down)[way])
 
-    proj = jnp.dot(nb[...], wg[:, hw:], preferred_element_type=jnp.float32)
+    proj = jnp.dot(nb[...], wg[...], preferred_element_type=jnp.float32)
     kt[z, :hw, :] = jnp.transpose(proj[:, :hw]).astype(jnp.bfloat16)
     kt[z, hw:hw + 16, :] = jnp.broadcast_to(sv[...].astype(jnp.float32), (16, rows)).astype(jnp.bfloat16)
     vb[z] = proj[:, hw:].astype(jnp.bfloat16)
@@ -206,7 +212,8 @@
             for piece in range(4):
                 kv_send(piece, way, 1).start()
 
-    qb[1] = jnp.dot(nb[...], wg[:, :hw], preferred_element_type=jnp.float32).astype(jnp.bfloat16)
+    arrived(wgq.at[pl.ds(0, nz * depth), :], qy_r.at[0])
+    qb[1] = jnp.dot(nb[...], wgq[...], preferred_element_type=jnp.float32).astype(jnp.bfloat16)
     query_copy = remote(qb.at[1], qb.at[0], x_s.at[0], x_r.at[0], across)
 
     @pl.when(yl == 1)
@@ -251,6 +258,9 @@
         def _():
             wo_send(way, step + 1).start()
 
+    other_out = wog.at[z, 1 - yl]
+    remote(other_out, other_out, o_s.at[0], o_r.at[0], across).wait_recv()
+
     @pl.when(yl == 1)
     def _():
         wo_send(0, 1).start()
@@ -333,12 +343,13 @@
         return remote(ref, ref, sems[0].at[0], sems[1].at[a * ny + b if sems is direct else 0], device)
 
     direct, handed = (a_s, a_r), (f_s, f_r)
-    att_sends = [att_copy(m, a, b, direct, row_device(a, b, False)) for a, b in reversed(others)]
+    att_sends = [att_copy(m, a, b, direct, row_device(a, b, False)) for a, b in [(1, 0), (3, 0), (0, 1), (2, 0), (1, 1), (3, 1), (2, 1)]]
     att_sends += [att_copy(m, 0, 0, handed, sibling)]
     for copy in att_sends:
         copy.start()
 
     arrived(wg.at[pl.ds(0, (2 * nz - 1) * depth), :], w_s.at[0])
+    arrived(wgq.at[pl.ds(0, (2 * nz - 1) * depth), :], q_s.at[0])
     arrived(xg.at[pl.ds(0, nm - 1)], tok_s.at[0])
     out_weight.wait_send()
 
@@ -367,7 +378,7 @@
         return jnp.dot(att[head], weight, preferred_element_type=jnp.float32)
 
     mixed = xg[m].astype(jnp.float32) + project(m)
-    for a, b in others:
+    for a, b in [(1, 0), (3, 0), (0, 1), (2, 0), (1, 1), (3, 1), (2, 1)]:
         head = tile(-a, b, False)
         att_copy(head, a, b, direct, sibling).wait_recv()
         att_copy(head, a, b, handed, sibling).start()
@@ -397,7 +408,8 @@
         scratch_shapes=[
             pltpu.VMEM((nm, rows, hw), jnp.bfloat16),
             pltpu.VMEM((rows, nm * hw), jnp.bfloat16),
-            pltpu.VMEM((2 * nz * depth, 3 * hw), jnp.bfloat16),
+            pltpu.VMEM((2 * nz * depth, 2 * hw), jnp.bfloat16),
+            pltpu.VMEM((2 * nz * depth, hw), jnp.bfloat16),
             pltpu.VMEM((nz, 2, depth, hw), jnp.bfloat16),
             pltpu.VMEM((1, nm * hw), jnp.float32),
             pltpu.VMEM((1, rows), jnp.int32),
@@ -417,6 +429,8 @@
             dma((1,)), dma((4,)),
             dma((1,)), dma((2, steps)),
             dma((1,)),
+            dma((1,)), dma((2, steps)),
+            dma((1,)),
             dma((4, 2)), dma((4, 2, steps - 1)),
             dma((3,)), dma((3,)),
             dma((1,)), dma((nx * ny,)),

time: 87.2 us -> 85 us (0.975)
  Pallas kernels: 85.2 us -> 83.2 us
    pallas_call x1, Pallas kernels: 85.2 us -> 83.2 us  [on_device(): pl.pallas_call(functools.partial(kernel, nz, nx, ny), out_shape=jax.Shape...]
where the time goes in v4:
time: 85 us; the launch traced here: 84.7 us
  Pallas kernels  83.2 us (98%)
  local copies, waits for them, and re-layouts  1.47 us (2%)
    pallas_call x1, Pallas kernels, on_device(): pl.pallas_call(functools.partial(kernel, nz, nx, ny), out_shape=jax.Shape...  83.2 us

profile of v4, /device:TPU:25, one launch (start us, length us, event | category | flops | bytes accessed | tf_op | source)
XLA Modules:
  0.0 84.7 jit_solution(2196688288073771304)
XLA Ops:
  0.0 83.2 %sublayer.1 = bf16[256,128]{1,0:T(8,128)(2,1)} custom-call(bf16[256,128]{1,0:T(8,128)(2,1)} %tok.1, f32[1,2048]{1,0:T(1,128)} %bitcast.2, bf16[64,128]{1,0:T(8,128)(2,1)} %wq.1, bf16[64,128]{1,0:T(8,128)(2,1)} %wk.1, bf16[64,128]{1,0:T(8,128)(2,1)} %wv.1, bf16[64,128]{1,0:T(8,128)(2,1)} %wo.1, f32[16]{0:T(128)} %slopes.1, s32[1,256]{1,0:T(1,128)} %bitcast.3), custom_call_target="tpu_custom_call" | custom-call | tf_op jit(solution)/shard_map/sublayer/pallas_call | solution.py:403
  83.3 1.5 %copy.10 = bf16[256,128]{1,0:T(8,128)(2,1)} copy(bf16[256,128]{1,0:T(8,128)(2,1)} %sublayer.1) | data formatting | bytes 131072

commit v5 on v4

--- a/solution.py
+++ b/solution.py
@@ -29,7 +29,8 @@
     nm = nx * ny * 2
     up_steps = nz // 2
     down_steps = nz - 1 - up_steps
-    stride = 2
+    origin = {1: 0, 2: 0, 3: 2, 4: 2, 5: 4, 6: 4, 7: 6, 8: 6}
+    hops = sorted(set(offset - origin[offset] for offset in origin))
     s = lax.axis_index("seq")
     m = lax.axis_index("mp")
     z = lax.rem(s, nz)
@@ -60,7 +61,7 @@
     others = [(a, b) for a in range(nx) for b in range(ny) if a or b]
 
     barrier = pltpu.get_barrier_semaphore()
-    greeted = [along(way * far) for far in range(1, stride + 1) for way in (1, -1)] + [across, sibling] + [row_device(a, b, False) for a, b in others]
+    greeted = [along(way * far) for far in hops for way in (1, -1)] + [across, sibling] + [row_device(a, b, False) for a, b in others]
     for device in greeted:
         pl.semaphore_signal(barrier, inc=1, device_id=device, device_id_type=MESH)
 
@@ -93,9 +94,8 @@
     def w_send(side, way, offset):
         buf, sent, came, _ = side
         sign = 1 - 2 * way
-        hops = min(offset, stride)
-        ref = shard(buf, yl, z - sign * (offset - hops))
-        return remote(ref, ref, sent.at[0], came.at[way, offset], along(sign * hops))
+        ref = shard(buf, yl, z - sign * origin[offset])
+        return remote(ref, ref, sent.at[0], came.at[way, offset], along(sign * (offset - origin[offset])))
 
     def w_hand(side, way, offset):
         buf, sent, _, handed = side
@@ -107,15 +107,17 @@
             for way in (0, 1):
                 if offset <= last_offset[way]:
                     arrived(shard(side[0], yl, z - (1 - 2 * way) * offset), side[2].at[way, offset])
-                    if offset + stride <= last_offset[way]:
-                        w_send(side, way, offset + stride).start()
+                    for later in range(last_offset[way], offset, -1):
+                        if origin[later] == offset:
+                            w_send(side, way, later).start()
                     w_hand(side, way, offset).start()
 
     last_offset = (up_steps, down_steps)
-    for first in range(1, stride + 1):
-        for side in (key_value, queries):
-            for way in (0, 1):
-                w_send(side, way, first).start()
+    for first in range(1, up_steps + 1):
+        if origin[first] == 0:
+            for side in (key_value, queries):
+                for way in (0, 1):
+                    w_send(side, way, first).start()
     for side in (key_value, queries):
         w_hand(side, 0, 0).start()
 
@@ -266,11 +268,11 @@
         wo_send(0, 1).start()
         wo_send(1, 1).start()
 
-    def kv_step(step, carry):
+    def kv_step(row, step, carry):
         before = step - 1
-        comes = [kv_comes(way, step) for way in (0, 1)]
-        went = [kv_goes(way, step) for way in (0, 1)]
-        goes = [kv_goes(way, step + 1) for way in (0, 1)]
+        comes = [kv_comes(way, step) if row else step <= last_offset[way] for way in (0, 1)]
+        went = [kv_goes(way, step) if row else step <= last_offset[way] for way in (0, 1)]
+        goes = [kv_goes(way, step + 1) if row else step + 1 <= last_offset[way] for way in (0, 1)]
         for index in range(4):
             for way in (0, 1):
                 @pl.when(comes[way])
@@ -287,12 +289,14 @@
 
             way, group = index // 2, 1 - index % 2
             block = ring(z - (1 - 2 * way) * before)
+            if group == 0 and row == 1:
+                continue
             if index == 1:
-                @pl.when((before == 0) & (yl == 0))
+                @pl.when(before == 0)
                 def _():
                     query_copy.wait_recv()
 
-            wanted = yl == 0 if group == 0 else block <= z
+            wanted = before >= 0 if group == 0 else block <= z
             if way == 1:
                 wanted = wanted & (before >= 1) & (before <= down_steps)
 
@@ -300,14 +304,21 @@
             def _():
                 attend(group, block)
 
-        for way in (0, 1):
-            @pl.when((yl == 1) & (step <= last_offset[way]))
+        for way in (0, 1) if row else ():
+            @pl.when(step <= last_offset[way])
             def _():
                 wo_step(way, step)
 
         return carry
 
-    lax.fori_loop(1, up_steps + 2, kv_step, 0)
+    @pl.when(yl == 0)
+    def _():
+        lax.fori_loop(1, up_steps + 2, functools.partial(kv_step, 0), 0)
+
+    @pl.when(yl == 1)
+    def _():
+        lax.fori_loop(1, up_steps + 2, functools.partial(kv_step, 1), 0)
+
 
     out_copy = remote(ob.at[0], ob.at[1], x_s.at[1], x_r.at[1], across)
     stat_copy = remote(sb.at[0], sb.at[1], x_s.at[2], x_r.at[2], across)

time: 85 us -> 84.5 us (level)
  no operation moved by 1% of the time
where the time goes in v5:
time: 84.5 us; the launch traced here: 84.3 us
  Pallas kernels  82.9 us (98%)
  local copies, waits for them, and re-layouts  1.47 us (2%)
    pallas_call x1, Pallas kernels, on_device(): pl.pallas_call(functools.partial(kernel, nz, nx, ny), out_shape=jax.Shape...  82.9 us

profile of v5, /device:TPU:25, one launch (start us, length us, event | category | flops | bytes accessed | tf_op | source)
XLA Modules:
  0.0 84.3 jit_solution(12632455951556046758)
XLA Ops:
  0.0 82.9 %sublayer.1 = bf16[256,128]{1,0:T(8,128)(2,1)} custom-call(bf16[256,128]{1,0:T(8,128)(2,1)} %tok.1, f32[1,2048]{1,0:T(1,128)} %bitcast.2, bf16[64,128]{1,0:T(8,128)(2,1)} %wq.1, bf16[64,128]{1,0:T(8,128)(2,1)} %wk.1, bf16[64,128]{1,0:T(8,128)(2,1)} %wv.1, bf16[64,128]{1,0:T(8,128)(2,1)} %wo.1, f32[16]{0:T(128)} %slopes.1, s32[1,256]{1,0:T(1,128)} %bitcast.3), custom_call_target="tpu_custom_call" | custom-call | tf_op jit(solution)/shard_map/sublayer/pallas_call | solution.py:414
  82.9 1.5 %copy.10 = bf16[256,128]{1,0:T(8,128)(2,1)} copy(bf16[256,128]{1,0:T(8,128)(2,1)} %sublayer.1) | data formatting | bytes 131072

commit v6 on v5

--- a/solution.py
+++ b/solution.py
@@ -142,24 +142,26 @@
         for copy in later:
             copy.start()
 
+    w_event(2, (key_value,))
     w_event(1, (key_value,))
-    w_event(2, (key_value,))
     arrived(xg.at[0], tok_r.at[1])
     tok_pass(0, 1)
+    w_event(2, (queries,))
+    w_event(1, (queries,))
     arrived(xg.at[pl.ds(0, nx - 1)], tok_r.at[0])
     for a in range(1, nx):
         tok_pass(a, 0)
-    w_event(1, (queries,))
-    w_event(2, (queries,))
+    w_event(4, (key_value,))
     w_event(3, (key_value,))
-    w_event(4, (key_value,))
+    w_event(4, (queries,))
+    w_event(3, (queries,))
     arrived(xg.at[pl.ds(0, nx - 1)], tok_r.at[2])
     for a in range(1, nx):
         tok_pass(a, 1)
-    w_event(3, (queries,))
-    w_event(4, (queries,))
+    w_event(6, (key_value,))
     w_event(5, (key_value,))
-    w_event(6, (key_value,))
+    w_event(6, (queries,))
+    w_event(5, (queries,))
     arrived(xg.at[pl.ds(0, nx * ny)], tok_r.at[3])
     square = jnp.zeros((rows, hw), jnp.float32)
     for h in range(nm):
@@ -171,12 +173,10 @@
         part = xg[h].astype(jnp.float32) * scale * gv[:, h * hw:(h + 1) * hw]
         nb[:, h * hw:(h + 1) * hw] = part.astype(jnp.bfloat16)
 
-    w_event(5, (queries,))
-    w_event(6, (queries,))
+    w_event(8, (key_value,))
     w_event(7, (key_value,))
-    w_event(8, (key_value,))
+    w_event(8, (queries,))
     w_event(7, (queries,))
-    w_event(8, (queries,))
     arrived(wg.at[pl.ds(0, nz * depth), :], wy_r.at[0])
 
     half = hw // 2

time: 84.5 us -> 83.5 us (0.988)
  Pallas kernels: 82.9 us -> 81.5 us
    pallas_call x1, Pallas kernels: 82.9 us -> 81.5 us  [on_device(): pl.pallas_call(functools.partial(kernel, nz, nx, ny), out_shape=jax.Shape...]
where the time goes in v6:
time: 83.5 us; the launch traced here: 83 us
  Pallas kernels  81.5 us (98%)
  local copies, waits for them, and re-layouts  1.47 us (2%)
    pallas_call x1, Pallas kernels, on_device(): pl.pallas_call(functools.partial(kernel, nz, nx, ny), out_shape=jax.Shape...  81.5 us

profile of v6, /device:TPU:25, one launch (start us, length us, event | category | flops | bytes accessed | tf_op | source)
XLA Modules:
  0.0 83.0 jit_solution(12083334323515459333)
XLA Ops:
  0.0 81.5 %sublayer.1 = bf16[256,128]{1,0:T(8,128)(2,1)} custom-call(bf16[256,128]{1,0:T(8,128)(2,1)} %tok.1, f32[1,2048]{1,0:T(1,128)} %bitcast.2, bf16[64,128]{1,0:T(8,128)(2,1)} %wq.1, bf16[64,128]{1,0:T(8,128)(2,1)} %wk.1, bf16[64,128]{1,0:T(8,128)(2,1)} %wv.1, bf16[64,128]{1,0:T(8,128)(2,1)} %wo.1, f32[16]{0:T(128)} %slopes.1, s32[1,256]{1,0:T(1,128)} %bitcast.3), custom_call_target="tpu_custom_call" | custom-call | tf_op jit(solution)/shard_map/sublayer/pallas_call | solution.py:414
  81.5 1.5 %copy.10 = bf16[256,128]{1,0:T(8,128)(2,1)} copy(bf16[256,128]{1,0:T(8,128)(2,1)} %sublayer.1) | data formatting | bytes 131072

commit v7 on v6

--- a/solution.py
+++ b/solution.py
@@ -113,7 +113,7 @@
                     w_hand(side, way, offset).start()
 
     last_offset = (up_steps, down_steps)
-    for first in range(1, up_steps + 1):
+    for first in range(up_steps, 0, -1):
         if origin[first] == 0:
             for side in (key_value, queries):
                 for way in (0, 1):

time: 83.5 us -> 82.9 us (level)
  no operation moved by 1% of the time
where the time goes in v7:
time: 82.9 us; the launch traced here: 82.7 us
  Pallas kernels  81.2 us (98%)
  local copies, waits for them, and re-layouts  1.47 us (2%)
    pallas_call x1, Pallas kernels, on_device(): pl.pallas_call(functools.partial(kernel, nz, nx, ny), out_shape=jax.Shape...  81.2 us

profile of v7, /device:TPU:25, one launch (start us, length us, event | category | flops | bytes accessed | tf_op | source)
XLA Modules:
  0.0 82.7 jit_solution(2577657379413751608)
XLA Ops:
  0.0 81.2 %sublayer.1 = bf16[256,128]{1,0:T(8,128)(2,1)} custom-call(bf16[256,128]{1,0:T(8,128)(2,1)} %tok.1, f32[1,2048]{1,0:T(1,128)} %bitcast.2, bf16[64,128]{1,0:T(8,128)(2,1)} %wq.1, bf16[64,128]{1,0:T(8,128)(2,1)} %wk.1, bf16[64,128]{1,0:T(8,128)(2,1)} %wv.1, bf16[64,128]{1,0:T(8,128)(2,1)} %wo.1, f32[16]{0:T(128)} %slopes.1, s32[1,256]{1,0:T(1,128)} %bitcast.3), custom_call_target="tpu_custom_call" | custom-call | tf_op jit(solution)/shard_map/sublayer/pallas_call | solution.py:414
  81.2 1.5 %copy.10 = bf16[256,128]{1,0:T(8,128)(2,1)} copy(bf16[256,128]{1,0:T(8,128)(2,1)} %sublayer.1) | data formatting | bytes 131072
